TPU v7x, 32 devices: a whole 2x2x4 slice. The times are simulated.
32 devices in a mesh: dp: 8 (over z, x), fsdp: 4 (over y, core).
Axes of the slice: x: 2, y: 2, z: 4, core: 2. Of those that a mesh axis runs over, the one named last changes fastest.
Arguments:
- pixels: bfloat16 [64, 256, 13, 64], P(('dp', 'fsdp')), may hold values from -6 to 6
- sensor: int32 [64], P(('dp', 'fsdp')), may hold values from 0 to 3
- band_wave: int32 [64, 13], P(('dp', 'fsdp')), may hold values from 0 to 31
- visible: int32 [64, 256], P(('dp', 'fsdp')), may hold values from 0 to 1023, as said below
- block_order: int32 [1024], replicated, may hold values from 0 to 1023, each once
- pre_gain: bfloat16 [768], P(('dp', 'fsdp')), may hold values from 0.5 to 1.5
- pre_shift: bfloat16 [768], P(('dp', 'fsdp')), may hold values from -1.1953125 to 1.1953125
- qkv_weight: bfloat16 [768, 2304], P(('dp', 'fsdp')), may hold values from -0.21875 to 0.21875
- out_weight: bfloat16 [768, 768], P(('dp', 'fsdp')), may hold values from -0.625 to 0.625
- mid_gain: bfloat16 [768], P(('dp', 'fsdp')), may hold values from 0.5 to 1.5
- mid_shift: bfloat16 [768], P(('dp', 'fsdp')), may hold values from -1.1953125 to 1.1953125
- up_weight: bfloat16 [768, 3072], P(('dp', 'fsdp')), may hold values from -0.21875 to 0.21875
- up_bias: bfloat16 [3072], P(('dp', 'fsdp')), may hold values from -1.1953125 to 1.1953125
- down_weight: bfloat16 [3072, 768], P(('dp', 'fsdp')), may hold values from -0.109375 to 0.109375
- down_bias: bfloat16 [768], P(('dp', 'fsdp')), may hold values from -1.1953125 to 1.1953125
- dec_weight: bfloat16 [768, 512], P(('dp', 'fsdp')), may hold values from -0.21875 to 0.21875
- dec_bias: bfloat16 [512], P(('dp', 'fsdp')), may hold values from -1.1953125 to 1.1953125
- mask_token: bfloat16 [512], P(('dp', 'fsdp')), may hold values from -6 to 6
- gen_tokens: bfloat16 [129, 128], P(None, ('dp', 'fsdp')), may hold values from -6 to 6
- gen_qkv: bfloat16 [128, 384], P(('dp', 'fsdp')), may hold values from -0.5 to 0.5
- gen_out: bfloat16 [128, 128], P(('dp', 'fsdp')), may hold values from -1 to 1
- gen_out_bias: bfloat16 [128], P(('dp', 'fsdp')), may hold values from -1.1953125 to 1.1953125
- gen_gain1: bfloat16 [128], P(('dp', 'fsdp')), may hold values from 0.5 to 1.5
- gen_shift1: bfloat16 [128], P(('dp', 'fsdp')), may hold values from -1.1953125 to 1.1953125
- gen_up: bfloat16 [128, 2048], P(('dp', 'fsdp')), may hold values from -0.5 to 0.5
- gen_up_bias: bfloat16 [2048], P(('dp', 'fsdp')), may hold values from -1.1953125 to 1.1953125
- gen_down: bfloat16 [2048, 128], P(('dp', 'fsdp')), may hold values from -0.125 to 0.125
- gen_down_bias: bfloat16 [128], P(('dp', 'fsdp')), may hold values from -1.1953125 to 1.1953125
- gen_gain2: bfloat16 [128], P(('dp', 'fsdp')), may hold values from 0.5 to 1.5
- gen_shift2: bfloat16 [128], P(('dp', 'fsdp')), may hold values from -1.1953125 to 1.1953125
- kernel_weight: bfloat16 [128, 49152], P(None, ('dp', 'fsdp')), may hold values from -0.0234375 to 0.0234375
- kernel_bias: bfloat16 [49152], P(('dp', 'fsdp')), may hold values from -0.119628906 to 0.119628906
- bias_weight: bfloat16 [128, 768], P(('dp', 'fsdp')), may hold values from -0.5 to 0.5
- cotangent: bfloat16 [64, 1024, 512], P(None, ('dp', 'fsdp')), may hold values from -6 to 6
Outputs:
- decoder_in: bfloat16 [64, 1024, 512], P(None, ('dp', 'fsdp'))
- grad_pixels: float32 [64, 256, 13, 64], P(('dp', 'fsdp'))
- grad_pre_gain: float32 [768], P(('dp', 'fsdp'))
- grad_pre_shift: float32 [768], P(('dp', 'fsdp'))
- grad_qkv_weight: float32 [768, 2304], P(('dp', 'fsdp'))
- grad_out_weight: float32 [768, 768], P(('dp', 'fsdp'))
- grad_mid_gain: float32 [768], P(('dp', 'fsdp'))
- grad_mid_shift: float32 [768], P(('dp', 'fsdp'))
- grad_up_weight: float32 [768, 3072], P(('dp', 'fsdp'))
- grad_up_bias: float32 [3072], P(('dp', 'fsdp'))
- grad_down_weight: float32 [3072, 768], P(('dp', 'fsdp'))
- grad_down_bias: float32 [768], P(('dp', 'fsdp'))
- grad_dec_weight: float32 [768, 512], P(('dp', 'fsdp'))
- grad_dec_bias: float32 [512], P(('dp', 'fsdp'))
- grad_mask_token: float32 [512], P(('dp', 'fsdp'))
- grad_gen_tokens: float32 [129, 128], P(None, ('dp', 'fsdp'))
- grad_gen_qkv: float32 [128, 384], P(('dp', 'fsdp'))
- grad_gen_out: float32 [128, 128], P(('dp', 'fsdp'))
- grad_gen_out_bias: float32 [128], P(('dp', 'fsdp'))
- grad_gen_gain1: float32 [128], P(('dp', 'fsdp'))
- grad_gen_shift1: float32 [128], P(('dp', 'fsdp'))
- grad_gen_up: float32 [128, 2048], P(('dp', 'fsdp'))
- grad_gen_up_bias: float32 [2048], P(('dp', 'fsdp'))
- grad_gen_down: float32 [2048, 128], P(('dp', 'fsdp'))
- grad_gen_down_bias: float32 [128], P(('dp', 'fsdp'))
- grad_gen_gain2: float32 [128], P(('dp', 'fsdp'))
- grad_gen_shift2: float32 [128], P(('dp', 'fsdp'))
- grad_kernel_weight: float32 [128, 49152], P(None, ('dp', 'fsdp'))
- grad_kernel_bias: float32 [49152], P(('dp', 'fsdp'))
- grad_bias_weight: float32 [128, 768], P(('dp', 'fsdp'))
Inputs may be any that keep to these rules, and one draw needn't show every extreme that they name: Each row of visible holds 256 different patch indices.
All inputs are finite; a program needn't handle non-finite values.
Results may differ from a plain program's by a relative error of at most 0.014.
Values may be sent and summed in bfloat16 or wider, within the bound.
A program may use at most 256 MiB of HBM per device.

v0:
```python
from functools import partial
import math

import jax
import jax.numpy as jnp
from jax import lax
from jax.sharding import PartitionSpec as P

HEADS = 12
WD = 128
GHEADS = 4
LAT = 128
NWAVE = 32
GRID = 32
PATCH = 1024


EPS = 1e-05
BAND_DROP = (0, 6, 9, 7)
HIGH = lax.Precision.HIGHEST


def sincos(values, count):
    freq = jnp.exp(jnp.arange(count, dtype=jnp.float32) * (-math.log(10000.0) / count))
    angle = values[..., None] * freq
    return jnp.concatenate([jnp.sin(angle), jnp.cos(angle)], axis=-1)


def norm_rows(rows, gain, shift):
    mean = jnp.mean(rows, axis=-1, keepdims=True)
    centred = rows - mean
    spread = jnp.mean(centred * centred, axis=-1, keepdims=True)
    return centred * lax.rsqrt(spread + EPS) * gain + shift


def exact_gelu(values):
    return jax.nn.gelu(values, approximate=False)


def band_valid(sensor, bands):
    drops = jnp.array(BAND_DROP, jnp.int32)
    picked = jnp.where(
        sensor[:, None] == jnp.arange(4, dtype=jnp.int32)[None, :], drops[None, :], 0
    )
    count = bands - jnp.sum(picked, axis=1)
    return (jnp.arange(bands, dtype=jnp.int32)[None, :] < count[:, None]).astype(jnp.float32)


def place_code(visible, width):
    row = (visible // GRID).astype(jnp.float32)
    col = (visible % GRID).astype(jnp.float32)
    return jnp.concatenate([sincos(row, width // 4), sincos(col, width // 4)], axis=-1)


def gen_core(
    wave_code,
    tokens,
    gen_qkv,
    gen_out,
    gen_out_bias,
    gen_gain1,
    gen_shift1,
    gen_up,
    gen_up_bias,
    gen_down,
    gen_down_bias,
    gen_gain2,
    gen_shift2,
):
    sequence = jnp.concatenate([tokens[:LAT], wave_code, tokens[LAT:]], axis=0)
    length = sequence.shape[0]
    width = sequence.shape[1]
    head_dim = width // GHEADS
    joint = jnp.dot(sequence, gen_qkv, precision=HIGH).reshape(length, 3, GHEADS, head_dim)
    scores = jnp.einsum("qhe,khe->hqk", joint[:, 0], joint[:, 1], precision=HIGH) / math.sqrt(
        head_dim
    )
    probs = jax.nn.softmax(scores, axis=-1)
    context = jnp.einsum("hqk,khe->qhe", probs, joint[:, 2], precision=HIGH).reshape(length, width)
    mixed = norm_rows(
        sequence + jnp.dot(context, gen_out, precision=HIGH) + gen_out_bias, gen_gain1, gen_shift1
    )
    hidden = jax.nn.gelu(jnp.dot(mixed, gen_up, precision=HIGH) + gen_up_bias, approximate=False)
    final = norm_rows(
        mixed + jnp.dot(hidden, gen_down, precision=HIGH) + gen_down_bias, gen_gain2, gen_shift2
    )
    feature = final[LAT : LAT + NWAVE] + sequence[LAT : LAT + NWAVE]
    return (feature, final[length - 1])


def own_part(full, dim):
    count = lax.axis_size("dp") * lax.axis_size("fsdp")
    index = lax.axis_index("dp") * lax.axis_size("fsdp") + lax.axis_index("fsdp")
    piece = full.shape[dim] // count
    return lax.dynamic_slice_in_dim(full, index * piece, piece, dim)


def tdot(left, right):
    return lax.dot_general(
        left, right, (((0,), (0,)), ((), ())), preferred_element_type=jnp.float32
    )


def ndot(left, right):
    return lax.dot_general(
        left, right, (((1,), (1,)), ((), ())), preferred_element_type=jnp.float32
    )


def on_device(
    pixels,
    sensor,
    band_wave,
    visible,
    block_order,
    pre_gain,
    pre_shift,
    qkv_weight,
    out_weight,
    mid_gain,
    mid_shift,
    up_weight,
    up_bias,
    down_weight,
    down_bias,
    dec_weight,
    dec_bias,
    mask_token,
    gen_tokens,
    gen_qkv,
    gen_out,
    gen_out_bias,
    gen_gain1,
    gen_shift1,
    gen_up,
    gen_up_bias,
    gen_down,
    gen_down_bias,
    gen_gain2,
    gen_shift2,
    kernel_weight,
    kernel_bias,
    bias_weight,
    cotangent,
):
    fetched = (
        lax.all_gather(pre_gain, ("dp", "fsdp"), axis=0, tiled=True),
        lax.all_gather(pre_shift, ("dp", "fsdp"), axis=0, tiled=True),
        lax.all_gather(qkv_weight, ("dp", "fsdp"), axis=0, tiled=True),
        lax.all_gather(out_weight, ("dp", "fsdp"), axis=0, tiled=True),
        lax.all_gather(mid_gain, ("dp", "fsdp"), axis=0, tiled=True),
        lax.all_gather(mid_shift, ("dp", "fsdp"), axis=0, tiled=True),
        lax.all_gather(up_weight, ("dp", "fsdp"), axis=0, tiled=True),
        lax.all_gather(up_bias, ("dp", "fsdp"), axis=0, tiled=True),
        lax.all_gather(down_weight, ("dp", "fsdp"), axis=0, tiled=True),
        lax.all_gather(down_bias, ("dp", "fsdp"), axis=0, tiled=True),
        lax.all_gather(dec_weight, ("dp", "fsdp"), axis=0, tiled=True),
        lax.all_gather(dec_bias, ("dp", "fsdp"), axis=0, tiled=True),
        lax.all_gather(mask_token, ("dp", "fsdp"), axis=0, tiled=True),
        lax.all_gather(gen_tokens, ("dp", "fsdp"), axis=1, tiled=True),
        lax.all_gather(gen_qkv, ("dp", "fsdp"), axis=0, tiled=True),
        lax.all_gather(gen_out, ("dp", "fsdp"), axis=0, tiled=True),
        lax.all_gather(gen_out_bias, ("dp", "fsdp"), axis=0, tiled=True),
        lax.all_gather(gen_gain1, ("dp", "fsdp"), axis=0, tiled=True),
        lax.all_gather(gen_shift1, ("dp", "fsdp"), axis=0, tiled=True),
        lax.all_gather(gen_up, ("dp", "fsdp"), axis=0, tiled=True),
        lax.all_gather(gen_up_bias, ("dp", "fsdp"), axis=0, tiled=True),
        lax.all_gather(gen_down, ("dp", "fsdp"), axis=0, tiled=True),
        lax.all_gather(gen_down_bias, ("dp", "fsdp"), axis=0, tiled=True),
        lax.all_gather(gen_gain2, ("dp", "fsdp"), axis=0, tiled=True),
        lax.all_gather(gen_shift2, ("dp", "fsdp"), axis=0, tiled=True),
        lax.all_gather(kernel_weight, ("dp", "fsdp"), axis=1, tiled=True),
        lax.all_gather(kernel_bias, ("dp", "fsdp"), axis=0, tiled=True),
        lax.all_gather(bias_weight, ("dp", "fsdp"), axis=0, tiled=True),
    )
    full_kernel = fetched[25]
    full_kernel_bias = fetched[26]
    full_bias_weight = fetched[27]
    (
        full_pre_gain,
        full_pre_shift,
        full_qkv,
        full_out,
        full_mid_gain,
        full_mid_shift,
        full_up,
        full_up_bias,
        full_down,
        full_down_bias,
        full_dec,
        full_dec_bias,
        full_mask,
    ) = fetched[:13]
    core32 = tuple((item.astype(jnp.float32) for item in fetched[13:25]))
    chips, seen, bands, pix = pixels.shape
    width = full_qkv.shape[0]
    head_dim = width // HEADS
    scale = 1.0 / math.sqrt(head_dim)
    dec_width = full_dec.shape[1]
    rows = chips * seen
    wave_code = lax.optimization_barrier(
        sincos(jnp.arange(NWAVE, dtype=jnp.float32), WD // 2).astype(jnp.bfloat16)
    ).astype(jnp.float32)
    (feature, source), core_back = jax.vjp(partial(gen_core, wave_code), *core32)
    feature_low = feature.astype(jnp.bfloat16)
    source_low = source.astype(jnp.bfloat16)
    conv_bias = jnp.dot(source_low[None, :], full_bias_weight, preferred_element_type=jnp.float32)[
        0
    ]
    kernels = (
        jnp.dot(feature_low, full_kernel, preferred_element_type=jnp.float32)
        + full_kernel_bias.astype(jnp.float32)[None, :]
    ).astype(jnp.bfloat16)
    valid = band_valid(sensor, bands)
    onehot = (band_wave[:, :, None] == jnp.arange(NWAVE, dtype=jnp.int32)[None, None, :]).astype(
        jnp.float32
    )
    place = place_code(visible, width)
    band_kernels = jnp.einsum(
        "cbw,wk->cbk", onehot.astype(jnp.bfloat16), kernels, preferred_element_type=jnp.float32
    ).astype(jnp.bfloat16)
    band_kernels = band_kernels.reshape(chips, bands, pix, width)
    masked = pixels * valid.astype(jnp.bfloat16)[:, None, :, None]
    embedded = jnp.einsum(
        "cvbp,cbpd->cvd", masked, band_kernels, preferred_element_type=jnp.float32
    )
    start = (embedded + conv_bias + place).reshape(rows, width)
    pre_gain32 = full_pre_gain.astype(jnp.float32)
    pre_shift32 = full_pre_shift.astype(jnp.float32)
    normed = norm_rows(start, pre_gain32, pre_shift32).astype(jnp.bfloat16)
    joint = jnp.dot(normed, full_qkv, preferred_element_type=jnp.float32).astype(jnp.bfloat16)
    joint = joint.reshape(chips, seen, 3, HEADS, head_dim)
    queries = joint[:, :, 0]
    keys = joint[:, :, 1]
    values = joint[:, :, 2]
    scores = (
        jnp.einsum("cqhe,ckhe->chqk", queries, keys, preferred_element_type=jnp.float32) * scale
    )
    peak = jnp.max(scores, axis=-1, keepdims=True)
    expd = jnp.exp(scores - peak)
    total = jnp.sum(expd, axis=-1, keepdims=True)
    probs = (expd / total).astype(jnp.bfloat16)
    log_total = peak + jnp.log(total)
    context = jnp.einsum("chqk,ckhe->cqhe", probs, values, preferred_element_type=jnp.float32)
    context = context.astype(jnp.bfloat16).reshape(rows, width)
    attended = jnp.dot(context, full_out, preferred_element_type=jnp.float32)
    middle = start + attended
    mid_gain32 = full_mid_gain.astype(jnp.float32)
    mid_shift32 = full_mid_shift.astype(jnp.float32)
    normed2 = norm_rows(middle, mid_gain32, mid_shift32).astype(jnp.bfloat16)
    upper = jnp.dot(normed2, full_up, preferred_element_type=jnp.float32) + full_up_bias.astype(
        jnp.float32
    )
    activ = exact_gelu(upper).astype(jnp.bfloat16)
    branch = jnp.dot(activ, full_down, preferred_element_type=jnp.float32) + full_down_bias.astype(
        jnp.float32
    )
    ending = (middle + branch).astype(jnp.bfloat16)
    decoded = jnp.dot(ending, full_dec, preferred_element_type=jnp.float32) + full_dec_bias.astype(
        jnp.float32
    )
    decoded = decoded.astype(jnp.bfloat16).reshape(chips, seen, dec_width)
    chip_ids = jnp.arange(chips, dtype=jnp.int32)[:, None]
    canvas = jnp.broadcast_to(full_mask, (chips, PATCH, dec_width))
    canvas = canvas.at[chip_ids, visible].set(decoded)
    ordered = jnp.take(canvas, block_order, axis=1)
    decoder_in = lax.all_to_all(ordered, ("dp", "fsdp"), split_axis=1, concat_axis=0, tiled=True)
    returned = lax.all_to_all(cotangent, ("dp", "fsdp"), split_axis=0, concat_axis=1, tiled=True)
    (
        full_pre_gain,
        full_pre_shift,
        full_qkv,
        full_out,
        full_mid_gain,
        full_mid_shift,
        full_up,
        full_up_bias,
        full_down,
        full_down_bias,
        full_dec,
        full_dec_bias,
        full_mask,
    ) = (
        lax.all_gather(pre_gain, ("dp", "fsdp"), axis=0, tiled=True),
        lax.all_gather(pre_shift, ("dp", "fsdp"), axis=0, tiled=True),
        lax.all_gather(qkv_weight, ("dp", "fsdp"), axis=0, tiled=True),
        lax.all_gather(out_weight, ("dp", "fsdp"), axis=0, tiled=True),
        lax.all_gather(mid_gain, ("dp", "fsdp"), axis=0, tiled=True),
        lax.all_gather(mid_shift, ("dp", "fsdp"), axis=0, tiled=True),
        lax.all_gather(up_weight, ("dp", "fsdp"), axis=0, tiled=True),
        lax.all_gather(up_bias, ("dp", "fsdp"), axis=0, tiled=True),
        lax.all_gather(down_weight, ("dp", "fsdp"), axis=0, tiled=True),
        lax.all_gather(down_bias, ("dp", "fsdp"), axis=0, tiled=True),
        lax.all_gather(dec_weight, ("dp", "fsdp"), axis=0, tiled=True),
        lax.all_gather(dec_bias, ("dp", "fsdp"), axis=0, tiled=True),
        lax.all_gather(mask_token, ("dp", "fsdp"), axis=0, tiled=True),
    )
    restored = jnp.zeros_like(returned).at[:, block_order].set(returned)
    seen_grad = jnp.take_along_axis(restored, visible[:, :, None], axis=1)
    grad_mask = jnp.sum(restored.astype(jnp.float32), axis=(0, 1)) - jnp.sum(
        seen_grad.astype(jnp.float32), axis=(0, 1)
    )
    grad_rows = seen_grad.reshape(rows, dec_width)
    grad_dec_weight = tdot(ending, grad_rows)
    grad_dec_bias = jnp.sum(grad_rows.astype(jnp.float32), axis=0)
    grad_ending = ndot(grad_rows, full_dec)
    grad_branch = grad_ending.astype(jnp.bfloat16)
    grad_down_bias = jnp.sum(grad_branch.astype(jnp.float32), axis=0)
    grad_down_weight = tdot(activ, grad_branch)
    grad_activ = ndot(grad_branch, full_down)
    gelu_out, gelu_back = jax.vjp(exact_gelu, upper)
    grad_upper = gelu_back(grad_activ)[0].astype(jnp.bfloat16)
    grad_up_bias = jnp.sum(grad_upper.astype(jnp.float32), axis=0)
    grad_up_weight = tdot(normed2, grad_upper)
    grad_normed2 = ndot(grad_upper, full_up)
    norm_out, norm_back = jax.vjp(norm_rows, middle, mid_gain32, mid_shift32)
    through_mid, grad_mid_gain, grad_mid_shift = norm_back(grad_normed2)
    grad_middle = grad_ending + through_mid
    grad_attended = grad_middle.astype(jnp.bfloat16)
    grad_out_weight = tdot(context, grad_attended)
    grad_context = (
        ndot(grad_attended, full_out).astype(jnp.bfloat16).reshape(chips, seen, HEADS, head_dim)
    )
    again_scores = (
        jnp.einsum("cqhe,ckhe->chqk", queries, keys, preferred_element_type=jnp.float32) * scale
    )
    probs_full = jnp.exp(again_scores - log_total)
    probs_low = probs_full.astype(jnp.bfloat16)
    grad_values = jnp.einsum(
        "chqk,cqhe->ckhe", probs_low, grad_context, preferred_element_type=jnp.float32
    ).astype(jnp.bfloat16)
    grad_probs = jnp.einsum(
        "cqhe,ckhe->chqk", grad_context, values, preferred_element_type=jnp.float32
    )
    row_dot = jnp.sum(probs_full * grad_probs, axis=-1, keepdims=True)
    grad_scores = (probs_full * (grad_probs - row_dot)).astype(jnp.bfloat16)
    grad_queries = (
        jnp.einsum("chqk,ckhe->cqhe", grad_scores, keys, preferred_element_type=jnp.float32) * scale
    ).astype(jnp.bfloat16)
    grad_keys = (
        jnp.einsum("chqk,cqhe->ckhe", grad_scores, queries, preferred_element_type=jnp.float32)
        * scale
    ).astype(jnp.bfloat16)
    grad_joint = jnp.stack([grad_queries, grad_keys, grad_values], axis=2).reshape(rows, 3 * width)
    grad_qkv_weight = tdot(normed, grad_joint)
    grad_normed = ndot(grad_joint, full_qkv)
    first_out, first_back = jax.vjp(norm_rows, start, pre_gain32, pre_shift32)
    through_pre, grad_pre_gain, grad_pre_shift = first_back(grad_normed)
    grad_start = grad_middle + through_pre
    grad_conv_part = jnp.sum(grad_start, axis=0)
    grad_embedded = grad_start.astype(jnp.bfloat16).reshape(chips, seen, width)
    grad_band = jnp.einsum(
        "cvbp,cvd->cbpd", masked, grad_embedded, preferred_element_type=jnp.float32
    )
    grad_band = grad_band.reshape(chips, bands, pix * width)
    grad_pixels = jnp.einsum(
        "cvd,cbpd->cvbp", grad_embedded, band_kernels, preferred_element_type=jnp.float32
    )
    grad_pixels = grad_pixels * valid[:, None, :, None]
    grad_kernels_part = jnp.einsum("cbw,cbk->wk", onehot, grad_band, precision=HIGH)
    kernel_sum, grad_conv = lax.psum((grad_kernels_part, grad_conv_part), ("dp", "fsdp"))
    kernel_low = kernel_sum.astype(jnp.bfloat16)
    own_low = own_part(kernel_low, 1)
    grad_kernel_weight = tdot(feature_low, own_low)
    grad_kernel_bias = jnp.sum(own_low.astype(jnp.float32), axis=0)
    grad_feature = ndot(kernel_low, full_kernel)
    grad_bias_weight = own_part(source_low.astype(jnp.float32)[:, None] * grad_conv[None, :], 0)
    grad_source = jnp.dot(full_bias_weight.astype(jnp.float32), grad_conv, precision=HIGH)
    core_grads = core_back((grad_feature, grad_source))
    summed = (
        lax.psum_scatter(grad_pre_gain, ("dp", "fsdp"), scatter_dimension=0, tiled=True),
        lax.psum_scatter(grad_pre_shift, ("dp", "fsdp"), scatter_dimension=0, tiled=True),
        lax.psum_scatter(grad_qkv_weight, ("dp", "fsdp"), scatter_dimension=0, tiled=True),
        lax.psum_scatter(grad_out_weight, ("dp", "fsdp"), scatter_dimension=0, tiled=True),
        lax.psum_scatter(grad_mid_gain, ("dp", "fsdp"), scatter_dimension=0, tiled=True),
        lax.psum_scatter(grad_mid_shift, ("dp", "fsdp"), scatter_dimension=0, tiled=True),
        lax.psum_scatter(grad_up_weight, ("dp", "fsdp"), scatter_dimension=0, tiled=True),
        lax.psum_scatter(grad_up_bias, ("dp", "fsdp"), scatter_dimension=0, tiled=True),
        lax.psum_scatter(grad_down_weight, ("dp", "fsdp"), scatter_dimension=0, tiled=True),
        lax.psum_scatter(grad_down_bias, ("dp", "fsdp"), scatter_dimension=0, tiled=True),
        lax.psum_scatter(grad_dec_weight, ("dp", "fsdp"), scatter_dimension=0, tiled=True),
        lax.psum_scatter(grad_dec_bias, ("dp", "fsdp"), scatter_dimension=0, tiled=True),
        lax.psum_scatter(grad_mask, ("dp", "fsdp"), scatter_dimension=0, tiled=True),
    )
    return (
        decoder_in,
        grad_pixels,
        summed[0],
        summed[1],
        summed[2],
        summed[3],
        summed[4],
        summed[5],
        summed[6],
        summed[7],
        summed[8],
        summed[9],
        summed[10],
        summed[11],
        summed[12],
        own_part(core_grads[0], 1),
        own_part(core_grads[1], 0),
        own_part(core_grads[2], 0),
        own_part(core_grads[3], 0),
        own_part(core_grads[4], 0),
        own_part(core_grads[5], 0),
        own_part(core_grads[6], 0),
        own_part(core_grads[7], 0),
        own_part(core_grads[8], 0),
        own_part(core_grads[9], 0),
        own_part(core_grads[10], 0),
        own_part(core_grads[11], 0),
        grad_kernel_weight,
        grad_kernel_bias,
        grad_bias_weight,
    )


def solution(mesh):
    in_specs = (
        P(("dp", "fsdp"), None, None, None),
        P(("dp", "fsdp")),
        P(("dp", "fsdp"), None),
        P(("dp", "fsdp"), None),
        P(),
        P(("dp", "fsdp")),
        P(("dp", "fsdp")),
        P(("dp", "fsdp"), None),
        P(("dp", "fsdp"), None),
        P(("dp", "fsdp")),
        P(("dp", "fsdp")),
        P(("dp", "fsdp"), None),
        P(("dp", "fsdp")),
        P(("dp", "fsdp"), None),
        P(("dp", "fsdp")),
        P(("dp", "fsdp"), None),
        P(("dp", "fsdp")),
        P(("dp", "fsdp")),
        P(None, ("dp", "fsdp")),
        P(("dp", "fsdp"), None),
        P(("dp", "fsdp"), None),
        P(("dp", "fsdp")),
        P(("dp", "fsdp")),
        P(("dp", "fsdp")),
        P(("dp", "fsdp"), None),
        P(("dp", "fsdp")),
        P(("dp", "fsdp"), None),
        P(("dp", "fsdp")),
        P(("dp", "fsdp")),
        P(("dp", "fsdp")),
        P(None, ("dp", "fsdp")),
        P(("dp", "fsdp")),
        P(("dp", "fsdp"), None),
        P(None, ("dp", "fsdp"), None),
    )
    out_specs = (
        P(None, ("dp", "fsdp"), None),
        P(("dp", "fsdp"), None, None, None),
        P(("dp", "fsdp")),
        P(("dp", "fsdp")),
        P(("dp", "fsdp"), None),
        P(("dp", "fsdp"), None),
        P(("dp", "fsdp")),
        P(("dp", "fsdp")),
        P(("dp", "fsdp"), None),
        P(("dp", "fsdp")),
        P(("dp", "fsdp"), None),
        P(("dp", "fsdp")),
        P(("dp", "fsdp"), None),
        P(("dp", "fsdp")),
        P(("dp", "fsdp")),
        P(None, ("dp", "fsdp")),
        P(("dp", "fsdp"), None),
        P(("dp", "fsdp"), None),
        P(("dp", "fsdp")),
        P(("dp", "fsdp")),
        P(("dp", "fsdp")),
        P(("dp", "fsdp"), None),
        P(("dp", "fsdp")),
        P(("dp", "fsdp"), None),
        P(("dp", "fsdp")),
        P(("dp", "fsdp")),
        P(("dp", "fsdp")),
        P(None, ("dp", "fsdp")),
        P(("dp", "fsdp")),
        P(("dp", "fsdp"), None),
    )
    return jax.shard_map(
        on_device, mesh=mesh, in_specs=in_specs, out_specs=out_specs, check_vma=False
    )
```

profile of v0, /device:TPU:0, one launch (start us, length us, event | category | flops | bytes accessed | tf_op | source)
XLA Modules:
  0.0 1251.7 jit_solution(14683441437408424234)
XLA Ops:
  18.2 85.2 %all-gather = bf16[32,4,129]{2,1,0:T(4,128)(2,1)S(1)} all-gather(bf16[1,4,129]{2,1,0:T(4,128)(2,1)S(1)} %bitcast.262), channel_id=1, replica_groups=mesh['dp'=8,'fsdp'=4] {'dp','fsdp'}, dimensions={0}, use_global_device_ids=true | all-gather | bytes 34056 | tf_op jit(solution)/shard_map/all_gather | solution.py:160
  109.0 53.6 %all-reduce.30 = (bf16[512]{0:T(512)(128)(2,1)}, bf16[2048]{0:T(1024)(128)(2,1)S(1)}, bf16[128]{0:T(256)(128)(2,1)S(1)}, bf16[128]{0:T(256)(128)(2,1)S(1)}, bf16...) all-reduce(bf16[512]{0:T(512)(128)(2,1)S(1)} %dynamic-update-slice,, ...), channel_id=1, replica_groups=mesh['dp'=8,'fsdp'=4] {'dp','fsdp'}, use_global_device_ids=true, to_apply=%add.6 | all-reduce | flops 10752 | bytes 43008
  162.8 40.9 %all-gather.1 = bf16[32,4,384]{2,1,0:T(4,128)(2,1)S(1)} all-gather(bf16[1,4,384]{2,1,0:T(4,128)(2,1)S(1)} %bitcast.261), channel_id=1, replica_groups=mesh['dp'=8,'fsdp'=4] {'dp','fsdp'}, dimensions={0}, use_global_device_ids=true | all-gather | bytes 101376 | tf_op jit(solution)/shard_map/all_gather | solution.py:161
  205.8 36.7 %all-gather.2 = bf16[32,4,128]{2,1,0:T(4,128)(2,1)S(1)} all-gather(bf16[1,4,128]{2,1,0:T(4,128)(2,1)S(1)} %bitcast.263), channel_id=1, replica_groups=mesh['dp'=8,'fsdp'=4] {'dp','fsdp'}, dimensions={0}, use_global_device_ids=true | all-gather | bytes 33792 | tf_op jit(solution)/shard_map/all_gather | solution.py:162
  244.2 39.8 %all-gather.3 = bf16[32,4,2048]{2,1,0:T(4,128)(2,1)S(1)} all-gather(bf16[1,4,2048]{2,1,0:T(4,128)(2,1)S(1)} %bitcast.259), channel_id=1, replica_groups=mesh['dp'=8,'fsdp'=4] {'dp','fsdp'}, dimensions={0}, use_global_device_ids=true | all-gather | bytes 540672 | tf_op jit(solution)/shard_map/all_gather | solution.py:166
  284.0 37.7 %all-gather.4 = bf16[32,1,1536]{2,1,0:T(2,128)(2,1)S(1)} all-gather(bf16[1,1,1536]{2,1,0:T(2,128)(2,1)S(1)} %reshape.500), channel_id=1, replica_groups=mesh['dp'=8,'fsdp'=4] {'dp','fsdp'}, dimensions={0}, use_global_device_ids=true | all-gather | bytes 101376 | tf_op jit(solution)/shard_map/all_gather | solution.py:173
  321.7 41.0 %all-gather.5 = bf16[32,4,768]{2,1,0:T(4,128)(2,1)} all-gather(bf16[1,4,768]{2,1,0:T(4,128)(2,1)S(1)} %bitcast.260), channel_id=1, replica_groups=mesh['dp'=8,'fsdp'=4] {'dp','fsdp'}, dimensions={0}, use_global_device_ids=true | all-gather | bytes 202752 | tf_op jit(solution)/shard_map/all_gather | solution.py:174
  370.4 39.1 %all_gather.98 = bf16[2048,128]{1,0:T(8,128)(2,1)S(1)} all-gather(bf16[64,128]{1,0:T(8,128)(2,1)} %param.61), channel_id=1, replica_groups=mesh['dp'=8,'fsdp'=4] {'dp','fsdp'}, dimensions={0}, use_global_device_ids=true | all-gather | bytes 540672 | tf_op jit(solution)/shard_map/all_gather | solution.py:168
  422.2 42.3 %all_gather.115 = bf16[768,512]{1,0:T(8,128)(2,1)} all-gather(bf16[24,512]{1,0:T(8,128)(2,1)S(1)} %copy-done.66), channel_id=1, replica_groups=mesh['dp'=8,'fsdp'=4] {'dp','fsdp'}, dimensions={0}, use_global_device_ids=true | all-gather | bytes 811008 | tf_op jit(solution)/shard_map/all_gather | solution.py:157
  469.1 73.8 %scatter_fusion.1 = bf16[2,1024,512]{2,0,1:T(2,128)(2,1)S(1)} fusion(bf16[2,1024,512]{2,0,1:T(2,128)(2,1)S(1)} %broadcast_in_dim.84, s32[1024]{0:T(1024)S(1)} %get-tuple-element.234, bf16[1024,2,512]{2,1,0:T(2,128)(2,1)} %bitcast.230), kind=kCustom, calls=%fused_computation.3 | custom fusion | bytes 6295552 | tf_op jit(solution)/shard_map/scatter | solution.py:298
  552.9 8.8 convolution_convert_fusion
  601.9 21.0 %multiply_convert_fusion.1 = (bf16[512,3072]{1,0:T(8,128)(2,1)}, f32[512,3072]{1,0:T(8,128)}, f32[512,3072]{1,0:T(8,128)}) fusion(f32[3072]{0:T(1024)S(1)} %convert_element_type.233, bf16[768,3072]{1,0:T(8,128)(2,1)} %all-gather.18.cloned.1.call-done, f32[512,768]{1,0:T(8,128)} %copy-done.4, f32[768]{0:T(1024)S(1)} %convert_element_type.231, ...), kind=kOutput, calls=%fused_computation.17 | convolution fusion | flops 2521694208 | bytes 22042624 | tf_op jit(solution)/shard_map/dot_general | solution.py:251
  632.2 8.7 convert_reduce_fusion
  660.8 7.7 multiply_reduce_fusion
  688.6 8.8 fusion.117
  697.5 8.2 fusion.98
  720.1 8.1 reshape.427
  728.3 10.5 convolution_bitcast_fusion
  738.7 133.6 %all-reduce.32 = (f32[768]{0:T(1024)}, f32[768]{0:T(1024)}, f32[768]{0:T(1024)}, f32[768]{0:T(1024)}, f32[3072]{0:T(1024)}, /*index=5*/f32[768]{0:T(1024)}, f32[...) all-reduce(f32[768]{0:T(1024)S(1)} %get-tuple-element.182, ...), channel_id=2, replica_groups=mesh['dp'=8,'fsdp'=4] {'dp','fsdp'}, use_global_device_ids=true, to_apply=%region_21.22.clone | all-reduce | flops 1581568 | bytes 9506816
  875.0 64.6 %scatter_fusion = bf16[2,1024,512]{2,1,0:T(8,128)(2,1)} fusion(bf16[2,1024,512]{2,1,0:T(8,128)(2,1)} %broadcast_in_dim.75, s32[512]{0:T(512)S(1)} %bitcast.223, bf16[512,512]{1,0:T(8,128)(2,1)S(1)} %fusion.30), kind=kCustom, calls=%fused_computation.2 | custom fusion | bytes 1576960 | tf_op jit(solution)/shard_map/scatter | solution.py:265
  944.6 7.5 gather_fusion
  960.1 10.0 fusion.132
  1019.7 83.0 %reduce-scatter.10.cloned.1.call-done = f32[24,3072]{1,0:T(8,128)} async-done(((f32[768,3072]{1,0:T(8,128)}), f32[24,3072]{1,0:T(8,128)}) %reduce-scatter.10.cloned.1.call-update) | async-done | bytes 294928 | tf_op jit(solution)/shard_map/reduce_scatter | solution.py:377
  1102.8 141.7 %reduce-scatter.12.cloned.1.call-done = f32[96,768]{1,0:T(8,128)} async-done(((f32[3072,768]{1,0:T(8,128)}), f32[96,768]{1,0:T(8,128)}) %reduce-scatter.12.cloned.1.call-update) | async-done | bytes 294928 | tf_op jit(solution)/shard_map/reduce_scatter | solution.py:379
  (486 shorter events, 222.9 us)
Async XLA Ops:
  7.2 545.7 %all-gather.12.cloned.1.call-start = ((), (), s32[]{:S(2)}) async-start(), calls=%async_computation.7 | async-start | bytes 12976128 | tf_op jit(solution)/shard_map/all_gather | solution.py:172
  7.9 563.8 %all-gather.14.cloned.1.call-start = ((), (), s32[]{:S(2)}) async-start(), calls=%async_computation.8 | async-start | bytes 3649536 | tf_op jit(solution)/shard_map/all_gather | solution.py:149
  8.7 589.3 %all-gather.16.cloned.1.call-start = ((), (), s32[]{:S(2)}) async-start(), calls=%async_computation.9 | async-start | bytes 1216512 | tf_op jit(solution)/shard_map/all_gather | solution.py:150
  9.4 592.5 %all-gather.18.cloned.1.call-start = ((), (), s32[]{:S(2)}) async-start(), calls=%async_computation.10 | async-start | bytes 4866048 | tf_op jit(solution)/shard_map/all_gather | solution.py:153
  10.2 152.6 %copy-start.96 = (bf16[4,384]{1,0:T(4,128)(2,1)S(1)}, bf16[4,384]{1,0:T(4,128)(2,1)}, u32[]{:S(2)}) copy-start(bf16[4,384]{1,0:T(4,128)(2,1)} %param.54) | copy-start | bytes 9220
  10.2 454.3 %all-to-all-start.1 = ((bf16[64,32,512]{2,1,0:T(8,128)(2,1)}), bf16[64,32,512]{2,1,0:T(8,128)(2,1)S(1)}, u32[]{:S(2)}, u32[]{:S(2)}) async-start(bf16[64,32,512]{2,1,0:T(8,128)(2,1)} %param.68), calls=%async_computation.1 | async-start | bytes 4194304 | tf_op jit(solution)/shard_map/all_to_all | solution.py:268
  17.5 605.5 %all-gather.20.cloned.1.call-start = ((), (), s32[]{:S(2)}) async-start(), calls=%async_computation.11 | async-start | bytes 4866048 | tf_op jit(solution)/shard_map/all_gather | solution.py:155
  18.1 1001.6 %reduce-scatter.14.cloned.1.call-start = ((), (), s32[]{:S(2)}) async-start(), calls=%async_computation.16 | async-start | bytes 1622016 | tf_op jit(solution)/shard_map/reduce_scatter | solution.py:381
  103.5 138.9 %copy-start.41 = (f32[128,128]{1,0:T(8,128)}, f32[128,128]{1,0:T(8,128)S(1)}, u32[]{:S(2)}) copy-start(f32[128,128]{1,0:T(8,128)S(1)} %slice.50) | copy-start | bytes 196612
  103.6 138.9 %copy-start.93 = (f32[1,128]{1,0:T(1,128)}, f32[1,128]{1,0:T(1,128)S(1)}, u32[]{:S(2)}) copy-start(f32[1,128]{1,0:T(1,128)S(1)} %slice.51) | copy-start | bytes 1540
  162.8 390.1 %copy-start.53 = (bf16[32,128]{1,0:T(8,128)(2,1)}, bf16[32,128]{1,0:T(8,128)(2,1)S(1)}, u32[]{:S(2)}) copy-start(bf16[32,128]{1,0:T(8,128)(2,1)S(1)} %pad_maximum_fusion.4) | copy-start | bytes 24580
  205.7 157.0 %copy-start.47 = (f32[4,32,161]{2,1,0:T(8,128)}, f32[4,32,161]{2,1,0:T(8,128)S(1)}, u32[]{:S(2)}) copy-start(f32[4,32,161]{2,1,0:T(8,128)S(1)} %fusion.53) | copy-start | bytes 247300
  205.8 161.7 %copy-start.98 = (bf16[768]{0:T(1024)(128)(2,1)S(1)}, bf16[768]{0:T(1024)(128)(2,1)}, u32[]{:S(2)}) copy-start(bf16[768]{0:T(1024)(128)(2,1)} %get-tuple-element.212) | copy-start | bytes 4612
  242.9 171.0 %copy-start.28 = (f32[161,128]{1,0:T(8,128)}, f32[161,128]{1,0:T(8,128)S(1)}, u32[]{:S(2)}) copy-start(f32[161,128]{1,0:T(8,128)S(1)} %get-tuple-element.257) | copy-start | bytes 247300
  242.9 171.0 %copy-start.57 = (f32[161]{0:T(256)}, f32[161]{0:T(256)S(1)}, u32[]{:S(2)}) copy-start(f32[161]{0:T(256)S(1)} %broadcast_multiply_fusion.5) | copy-start | bytes 1936
  243.1 170.8 %copy-start.59 = (f32[161]{0:T(256)}, f32[161]{0:T(256)S(1)}, u32[]{:S(2)}) copy-start(f32[161]{0:T(256)S(1)} %fusion.95) | copy-start | bytes 1936
  415.3 291.1 %copy-start.52 = (f32[161,128]{1,0:T(8,128)}, f32[161,128]{1,0:T(8,128)S(1)}, u32[]{:S(2)}) copy-start(f32[161,128]{1,0:T(8,128)S(1)} %multiply_add_fusion.1) | copy-start | bytes 247300
  632.2 387.5 %reduce-scatter.8.cloned.1.call-start = ((), (), s32[]{:S(2)}) async-start(), calls=%async_computation.13 | async-start | bytes 2433024 | tf_op jit(solution)/shard_map/reduce_scatter | solution.py:374
  660.5 359.2 %reduce-scatter.6.cloned.1.call-start = ((), (), s32[]{:S(2)}) async-start(), calls=%async_computation.12 | async-start | bytes 7299072 | tf_op jit(solution)/shard_map/reduce_scatter | solution.py:373
  688.2 414.6 %reduce-scatter.10.cloned.1.call-start = ((), (), s32[]{:S(2)}) async-start(), calls=%async_computation.14 | async-start | bytes 9732096 | tf_op jit(solution)/shard_map/reduce_scatter | solution.py:377
  697.5 547.0 %reduce-scatter.12.cloned.1.call-start = ((), (), s32[]{:S(2)}) async-start(), calls=%async_computation.15 | async-start | bytes 9732096 | tf_op jit(solution)/shard_map/reduce_scatter | solution.py:379
  738.7 134.2 %copy-start.27 = (bf16[768,512]{1,0:T(8,128)(2,1)S(1)}, bf16[768,512]{1,0:T(8,128)(2,1)}, u32[]{:S(2)}) copy-start(bf16[768,512]{1,0:T(8,128)(2,1)} %all_gather.115) | copy-start | bytes 2359300
  738.7 134.2 %copy-start.46 = (bf16[512,768]{1,0:T(8,128)(2,1)S(1)}, bf16[512,768]{1,0:T(8,128)(2,1)}, u32[]{:S(2)}) copy-start(bf16[512,768]{1,0:T(8,128)(2,1)} %copy-done.45) | copy-start | bytes 2359300
  956.7 61.0 %all-to-all-start = ((bf16[2,1024,512]{2,0,1:T(2,128)(2,1)}), bf16[2,1024,512]{2,0,1:T(2,128)(2,1)S(1)}, u32[]{:S(2)}, u32[]{:S(2)}) async-start(bf16[2,1024,512]{2,0,1:T(2,128)(2,1)} %fusion.16), calls=%async_computation | async-start | bytes 4194304 | tf_op jit(solution)/shard_map/all_to_all | solution.py:267
  (113 other events, 2952.7 us)
Sparse Core Ops, SparseCore 0:
  11.0 122.9 all-gather.11
  136.9 58.3 all-gather.13
  198.2 52.8 all-gather.15
  253.9 63.3 all-gather.17
  320.0 64.9 all-gather.19
  632.3 93.6 reduce-scatter.13
  731.9 103.3 reduce-scatter.7
  842.4 118.8 reduce-scatter.5
  967.8 134.9 reduce-scatter.9
  1110.1 134.3 reduce-scatter.11
where the time goes:
time: 1270 us; the launch traced here: 1250 us
  blocking collectives  550 us (43%)
  local copies, waits for them, and re-layouts  242 us (19%)
  waiting for transfers between devices  228 us (18%)
  matrix products  164 us (13%)
  other arithmetic  39.7 us (3%)
  between operations  16.5 us (1%)
    unnamed x2, blocking collectives  187 us
    reduce_scatter x1, waiting for transfers between devices, on_device(): lax.psum_scatter(grad_down_weight, ('dp', 'fsdp'), scatter_dimension=0, t...  142 us
    all_gather x1, blocking collectives, on_device(): lax.all_gather(gen_tokens, ('dp', 'fsdp'), axis=1, tiled=True)  85.2 us
    reduce_scatter x1, waiting for transfers between devices, on_device(): lax.psum_scatter(grad_up_weight, ('dp', 'fsdp'), scatter_dimension=0, til...  83 us
    scatter x2, local copies, waits for them, and re-layouts, on_device(): restored = jnp.zeros_like(returned).at[:, block_order].set(returned)  75.6 us
    scatter x2, local copies, waits for them, and re-layouts, on_device(): canvas = canvas.at[chip_ids, visible].set(decoded)  69.6 us
    all_gather x1, blocking collectives, on_device(): lax.all_gather(dec_weight, ('dp', 'fsdp'), axis=0, tiled=True)  42.3 us
    all_gather x1, blocking collectives, on_device(): lax.all_gather(bias_weight, ('dp', 'fsdp'), axis=0, tiled=True)  41 us
  transfers between devices with their start and end apart: 12, of which 2 were waited for; matrix products, arithmetic and copies ran while one was open for 34% of the time, Pallas kernels for 0%

commit v1 on v0

--- a/solution.py
+++ b/solution.py
@@ -4,6 +4,8 @@
 import jax
 import jax.numpy as jnp
 from jax import lax
+from jax.experimental import pallas as pl
+from jax.experimental.pallas import tpu as pltpu
 from jax.sharding import PartitionSpec as P
 
 HEADS = 12
@@ -16,6 +18,7 @@
 
 
 EPS = 1e-05
+AXES = ("dp", "fsdp")
 BAND_DROP = (0, 6, 9, 7)
 HIGH = lax.Precision.HIGHEST
 
@@ -107,7 +110,460 @@
     )
 
 
-def on_device(
+MESH_ID = pl.DeviceIdType.MESH
+ANY = pl.BlockSpec(memory_space=pl.ANY)
+VMEM = pl.BlockSpec(memory_space=pltpu.VMEM)
+
+
+class Net:
+    def __init__(self, planes):
+        dp, fs = lax.axis_index("dp"), lax.axis_index("fsdp")
+        self.planes = planes
+        self.z, self.x = lax.div(dp, 2), lax.rem(dp, 2)
+        self.y, self.c = lax.div(fs, 2), lax.rem(fs, 2)
+        self.sib = self.at(self.z, self.x, self.y, 1 - self.c)
+        self.nx = self.at(self.z, 1 - self.x, self.y, self.c)
+        self.ny = self.at(self.z, self.x, 1 - self.y, self.c)
+
+    def at(self, z, x, y, c):
+        return (z * 2 + x, y * 2 + c)
+
+    def plane(self, k):
+        return lax.rem(self.z + k, self.planes)
+
+    def zpeer(self, k):
+        return self.at(self.plane(k), self.x, self.y, self.c)
+
+    def chip(self, k, dx=0, dy=0):
+        x = 1 - self.x if dx else self.x
+        y = 1 - self.y if dy else self.y
+        return self.plane(k) * 4 + x * 2 + y
+
+    def greet(self):
+        barrier = pltpu.get_barrier_semaphore()
+        partners = [self.sib, self.nx, self.ny]
+        partners += [self.zpeer(k) for k in range(1, self.planes)]
+        for partner in partners:
+            pl.semaphore_signal(barrier, inc=1, device_id=partner, device_id_type=MESH_ID)
+        pl.semaphore_wait(barrier, len(partners))
+
+
+class Wires:
+    def __init__(self, send, recv):
+        self.send, self.recv, self.used, self.started = send, recv, 0, []
+
+    def push(self, src, dst, device):
+        index = self.used
+        self.used += 1
+        copy = pltpu.make_async_remote_copy(
+            src_ref=src,
+            dst_ref=dst,
+            send_sem=self.send.at[index],
+            recv_sem=self.recv.at[index],
+            device_id=device,
+            device_id_type=MESH_ID,
+        )
+        copy.start()
+        self.started.append(copy)
+        return copy
+
+    def drain(self):
+        for copy in self.started:
+            copy.wait_send()
+
+
+class Gather:
+    def __init__(self, net, wires, own, piece):
+        self.net, self.wires, self.own, self.piece = net, wires, own, piece
+        self.z_in, self.first, self.second, self.twins = {}, {}, {}, []
+
+    def near(self, h):
+        return self.net.ny if h else self.net.nx
+
+    def far(self, h):
+        return self.net.nx if h else self.net.ny
+
+    def share(self, chip, h, src=None):
+        spot = self.piece(chip, h)
+        self.twins.append(self.wires.push(spot if src is None else src, spot, self.net.sib))
+
+    def begin(self):
+        for k in range(1, self.net.planes):
+            for h in range(2):
+                spot = self.piece(self.net.chip(0), h)
+                self.z_in[k, h] = self.wires.push(self.own(h), spot, self.net.zpeer(k))
+        self.spread(0)
+
+    def spread(self, k):
+        back = (self.net.planes - k) % self.net.planes
+        for h in range(2):
+            if k:
+                self.z_in[k, h].wait_recv()
+            spot = self.piece(self.net.chip(back), h)
+            src = self.own(h) if k == 0 else spot
+            self.first[k, h] = self.wires.push(src, spot, self.near(h))
+            self.second[k, h, 0] = self.wires.push(src, spot, self.far(h))
+            self.share(self.net.chip(back), h, src)
+
+    def relay(self, k):
+        back = (self.net.planes - k) % self.net.planes
+        for h in range(2):
+            self.first[k, h].wait_recv()
+            chip = self.net.chip(back, dx=h == 0, dy=h == 1)
+            spot = self.piece(chip, h)
+            self.second[k, h, 1] = self.wires.push(spot, spot, self.far(h))
+            self.share(chip, h)
+
+    def close(self, k):
+        back = (self.net.planes - k) % self.net.planes
+        for h in range(2):
+            for hop in range(2):
+                self.second[k, h, hop].wait_recv()
+                chip = self.net.chip(back, dx=hop == 1 or h == 1, dy=hop == 1 or h == 0)
+                self.share(chip, h)
+
+    def finish(self):
+        for copy in self.twins:
+            copy.wait_recv()
+
+
+def gather_copies(planes):
+    return 2 * (planes - 1) + 4 * planes + 2 * planes + 8 * planes
+
+
+def run_gathers(gathers, planes):
+    for item in gathers:
+        item.begin()
+    for k in range(planes):
+        for item in gathers:
+            if k:
+                item.spread(k)
+            item.relay(k)
+    for k in range(planes):
+        for item in gathers:
+            item.close(k)
+    for item in gathers:
+        item.finish()
+
+
+def small_gather_kernel(planes, src, out, send, recv, local):
+    net = Net(planes)
+    net.greet()
+    wires = Wires(send, recv)
+    half = src.shape[0] // 2
+    own = lambda h: src.at[pl.ds(h * half, half)]
+    piece = lambda chip, h: out.at[chip * 2 + net.c, pl.ds(h * half, half)]
+    here = pltpu.make_async_copy(src, out.at[net.chip(0) * 2 + net.c], local)
+    here.start()
+    run_gathers([Gather(net, wires, own, piece)], planes)
+    here.wait()
+    wires.drain()
+
+
+def small_gather(packed, planes, devices):
+    copies = gather_copies(planes)
+    return pl.pallas_call(
+        partial(small_gather_kernel, planes),
+        out_shape=jax.ShapeDtypeStruct((devices,) + packed.shape, packed.dtype),
+        in_specs=[VMEM],
+        out_specs=VMEM,
+        scratch_shapes=[
+            pltpu.SemaphoreType.DMA((copies,)),
+            pltpu.SemaphoreType.DMA((copies,)),
+            pltpu.SemaphoreType.DMA,
+        ],
+        compiler_params=pltpu.CompilerParams(collective_id=0, has_side_effects=True),
+    )(packed)
+
+
+def weight_gather_kernel(
+    planes, wide, down, table, wide_out, down_out, table_out, fresh, joined, send, recv, local
+):
+    net = Net(planes)
+    net.greet()
+    wires = Wires(send, recv)
+    rows = wide.shape[0]
+    cols = wide.shape[1] // 2
+    quarter = cols // 2
+    mine = pl.ds(pl.multiple_of(net.c * cols, 128), cols)
+    theirs = pl.ds(pl.multiple_of((1 - net.c) * cols, 128), cols)
+    pair = wires.push(wide.at[:, theirs], fresh, net.sib)
+    t_rows, t_cols = table.shape
+    t_half = t_cols // 2
+    t_own = lambda h: table.at[:, pl.ds(h * t_half, t_half)]
+    t_piece = lambda chip, h: table_out.at[
+        :, pl.ds(pl.multiple_of((chip * 2 + net.c) * t_cols + h * t_half, 128), t_half)
+    ]
+    d_rows = down.shape[0]
+    d_half = d_rows // 2
+    d_own = lambda h: down.at[pl.ds(h * d_half, d_half)]
+    d_piece = lambda chip, h: down_out.at[
+        pl.ds(pl.multiple_of((chip * 2 + net.c) * d_rows + h * d_half, 16), d_half)
+    ]
+    w_own = lambda h: joined.at[:, pl.ds(h * quarter, quarter)]
+    w_piece = lambda chip, h: wide_out.at[
+        pl.ds(pl.multiple_of(chip * 2 * rows, 16), 2 * rows),
+        pl.ds(pl.multiple_of((net.c * 2 + h) * quarter, 128), quarter),
+    ]
+    t_gather = Gather(net, wires, t_own, t_piece)
+    d_gather = Gather(net, wires, d_own, d_piece)
+    w_gather = Gather(net, wires, w_own, w_piece)
+    here = []
+    for own, piece in ((t_own, t_piece), (d_own, d_piece)):
+        for h in range(2):
+            here.append(pltpu.make_async_copy(own(h), piece(net.chip(0), h), local.at[len(here)]))
+            here[-1].start()
+    t_gather.begin()
+    d_gather.begin()
+    pair.wait_recv()
+    own32 = wide[:, mine].astype(jnp.float32)
+    sib32 = fresh[...].astype(jnp.float32)
+    first = net.c == 0
+    joined[...] = jnp.concatenate(
+        [jnp.where(first, own32, sib32), jnp.where(first, sib32, own32)], axis=0
+    ).astype(joined.dtype)
+    for h in range(2):
+        here.append(pltpu.make_async_copy(w_own(h), w_piece(net.chip(0), h), local.at[len(here)]))
+        here[-1].start()
+    w_gather.begin()
+    gathers = [t_gather, d_gather, w_gather]
+    for k in range(planes):
+        for item in gathers:
+            if k:
+                item.spread(k)
+            item.relay(k)
+    for k in range(planes):
+        for item in gathers:
+            item.close(k)
+    for item in gathers:
+        item.finish()
+    for copy in here:
+        copy.wait()
+    wires.drain()
+
+
+def weight_gather(wide, down, table, planes, devices):
+    copies = 3 * gather_copies(planes) + 1
+    rows, cols = wide.shape
+    low = wide.dtype
+    return pl.pallas_call(
+        partial(weight_gather_kernel, planes),
+        out_shape=(
+            jax.ShapeDtypeStruct((rows * devices, cols), low),
+            jax.ShapeDtypeStruct((down.shape[0] * devices, down.shape[1]), low),
+            jax.ShapeDtypeStruct((table.shape[0], table.shape[1] * devices), low),
+        ),
+        in_specs=[VMEM] * 3,
+        out_specs=[ANY] * 3,
+        scratch_shapes=[
+            pltpu.VMEM((rows, cols // 2), low),
+            pltpu.VMEM((2 * rows, cols // 2), low),
+            pltpu.SemaphoreType.DMA((copies,)),
+            pltpu.SemaphoreType.DMA((copies,)),
+            pltpu.SemaphoreType.DMA((6,)),
+        ],
+        compiler_params=pltpu.CompilerParams(
+            collective_id=1, has_side_effects=True, vmem_limit_bytes=40 * 2**20
+        ),
+    )(wide, down, table)
+
+
+class Reduce:
+    def __init__(self, net, wires, part, held, near_in, far_in, z_in):
+        self.net, self.wires, self.part, self.held = net, wires, part, held
+        self.near_in, self.far_in, self.z_in = near_in, far_in, z_in
+        self.pairs, self.near, self.far, self.along = {}, {}, {}, {}
+
+    def add(self, spot, other):
+        size = 16 if spot.shape[0] % 16 == 0 else 8
+
+        def some(i, _):
+            at = pl.ds(pl.multiple_of(i * size, size), size)
+            total = spot[at].astype(jnp.float32) + other[at].astype(jnp.float32)
+            spot[at] = total.astype(spot.dtype)
+            return 0
+
+        lax.fori_loop(0, spot.shape[0] // size, some, 0)
+
+    def begin(self, k):
+        for dx in range(2):
+            for dy in range(2):
+                for h in range(2):
+                    chip = self.net.chip(k, dx, dy)
+                    self.pairs[k, dx, dy, h] = self.wires.push(
+                        self.part(chip, 1 - self.net.c, h), self.held.at[chip, h], self.net.sib
+                    )
+
+    def stage0(self, k):
+        for dx, dy in ((1, 1), (0, 1), (1, 0), (0, 0)):
+            for h in range(2):
+                self.pairs[k, dx, dy, h].wait_recv()
+                chip = self.net.chip(k, dx, dy)
+                self.add(self.held.at[chip, h], self.part(chip, self.net.c, h))
+                if (dy if h == 0 else dx) == 1:
+                    other = dx if h == 0 else dy
+                    self.near[k, h, other] = self.wires.push(
+                        self.held.at[chip, h],
+                        self.near_in.at[k, h, other],
+                        self.net.ny if h == 0 else self.net.nx,
+                    )
+
+    def stage1(self, k):
+        for h in range(2):
+            for other in (1, 0):
+                self.near[k, h, other].wait_recv()
+                chip = self.net.chip(k, other, 0) if h == 0 else self.net.chip(k, 0, other)
+                self.add(self.held.at[chip, h], self.near_in.at[k, h, other])
+                if other:
+                    self.far[k, h] = self.wires.push(
+                        self.held.at[chip, h],
+                        self.far_in.at[k, h],
+                        self.net.nx if h == 0 else self.net.ny,
+                    )
+
+    def stage2(self, k):
+        for h in range(2):
+            self.far[k, h].wait_recv()
+            spot = self.held.at[self.net.chip(k), h]
+            self.add(spot, self.far_in.at[k, h])
+            if k:
+                self.along[k, h] = self.wires.push(spot, self.z_in.at[k - 1, h], self.net.zpeer(k))
+
+    def total(self, h):
+        value = self.held[self.net.chip(0), h].astype(jnp.float32)
+        for k in range(1, self.net.planes):
+            self.along[k, h].wait_recv()
+            value = value + self.z_in[k - 1, h].astype(jnp.float32)
+        return value
+
+
+def reduce_copies(planes):
+    return 8 * planes + 4 * planes + 2 * planes + 2 * (planes - 1)
+
+
+def reduce_scratch(planes, rows, cols, dtype):
+    return [
+        pltpu.VMEM((planes * 4, 2, rows, cols), dtype),
+        pltpu.VMEM((planes, 2, 2, rows, cols), dtype),
+        pltpu.VMEM((planes, 2, rows, cols), dtype),
+        pltpu.VMEM((planes - 1, 2, rows, cols), dtype),
+    ]
+
+
+def grad_reduce_kernel(planes, steps, *refs):
+    wide, down, table, vec, conv, weight = refs[:6]
+    wide_out, down_out, table_out, vec_out, all_out = refs[6:11]
+    scratch = refs[11:27]
+    final, hand, box, send, recv = refs[27:]
+    net = Net(planes)
+    net.greet()
+    wires = Wires(send, recv)
+    w_rows, w_cols = final.shape[1:]
+    d_rows = down_out.shape[0] // 2
+    t_cols = table_out.shape[1] // 2
+    w_part = lambda chip, c, h: wide.at[
+        pl.ds(pl.multiple_of(chip * w_rows, 16), w_rows),
+        pl.ds(pl.multiple_of((c * 2 + h) * w_cols, 128), w_cols),
+    ]
+    d_part = lambda chip, c, h: down.at[
+        pl.ds(pl.multiple_of(((chip * 2 + c) * 2 + h) * d_rows, 16), d_rows)
+    ]
+    t_part = lambda chip, c, h: table.at[
+        :, pl.ds(pl.multiple_of(((chip * 2 + c) * 2 + h) * t_cols, 128), t_cols)
+    ]
+    v_part = lambda chip, c, h: vec.at[chip, c, h]
+    items = [
+        Reduce(net, wires, part, *scratch[i * 4 : i * 4 + 4])
+        for i, part in enumerate((t_part, v_part, w_part, d_part))
+    ]
+    order = list(range(1, planes)) + [0]
+    units = [(item, k) for item in items for k in order]
+    for item, k in units:
+        item.begin(k)
+    for t in range(len(units) + 2):
+        if t < len(units):
+            units[t][0].stage0(units[t][1])
+        if 0 <= t - 1 < len(units):
+            units[t - 1][0].stage1(units[t - 1][1])
+        if 0 <= t - 2 < len(units):
+            units[t - 2][0].stage2(units[t - 2][1])
+    tables, vecs, wides, downs = items
+    for h in range(2):
+        table_out[:, pl.ds(h * t_cols, t_cols)] = tables.total(h).astype(table_out.dtype)
+    box[0, pl.ds(0, table.shape[0])] = lax.dot_general(
+        table_out[...], weight[...], (((1,), (1,)), ((), ())), preferred_element_type=jnp.float32
+    )
+    box[0, pl.ds(table.shape[0], conv.shape[0])] = conv[...]
+    peers = [net.sib, net.nx, net.ny]
+    for bit in range(steps):
+        step = 1 << bit
+        up = lax.rem(lax.div(net.z, step), 2) == 0
+        peers.append(net.at(jnp.where(up, net.z + step, net.z - step), net.x, net.y, net.c))
+    for i, peer in enumerate(peers):
+        hop = wires.push(box.at[2 * i], box.at[2 * i + 1], peer)
+        hop.wait_recv()
+        box[2 * i + 2] = box[2 * i] + box[2 * i + 1]
+    all_out[...] = box[2 * len(peers)]
+    for h in range(2):
+        vec_out[h] = vecs.total(h)
+    for h in range(2):
+        final[h] = wides.total(h)
+    half = w_rows // 2
+    mine = pl.ds(pl.multiple_of(net.c * half, 8), half)
+    theirs = pl.ds(pl.multiple_of((1 - net.c) * half, 8), half)
+    swaps = [
+        wires.push(final.at[h, theirs], hand.at[h], net.sib) for h in range(2)
+    ]
+    for h in range(2):
+        down_out[pl.ds(h * d_rows, d_rows)] = downs.total(h)
+    for h in range(2):
+        own = pl.ds(pl.multiple_of((net.c * 2 + h) * w_cols, 128), w_cols)
+        wide_out[:, own] = final[h, mine]
+    for h in range(2):
+        swaps[h].wait_recv()
+        other = pl.ds(pl.multiple_of(((1 - net.c) * 2 + h) * w_cols, 128), w_cols)
+        wide_out[:, other] = hand[h]
+    wires.drain()
+
+
+def grad_reduce(wide, down, table, vec, conv, weight, planes):
+    devices = planes * 8
+    low = wide.dtype
+    steps = (planes - 1).bit_length()
+    w_rows, w_cols = wide.shape[0] // (devices // 2), wide.shape[1] // 4
+    d_rows = down.shape[0] // devices // 2
+    t_cols = table.shape[1] // devices // 2
+    copies = 4 * reduce_copies(planes) + 2 + 3 + steps
+    box = (table.shape[0] + conv.shape[0], conv.shape[1])
+    return pl.pallas_call(
+        partial(grad_reduce_kernel, planes, steps),
+        out_shape=(
+            jax.ShapeDtypeStruct((w_rows // 2, wide.shape[1]), jnp.float32),
+            jax.ShapeDtypeStruct((2 * d_rows, down.shape[1]), jnp.float32),
+            jax.ShapeDtypeStruct((table.shape[0], 2 * t_cols), low),
+            jax.ShapeDtypeStruct(vec.shape[2:], jnp.float32),
+            jax.ShapeDtypeStruct(box, jnp.float32),
+        ),
+        in_specs=[VMEM] * 6,
+        out_specs=[VMEM] * 5,
+        scratch_shapes=reduce_scratch(planes, table.shape[0], t_cols, low)
+        + reduce_scratch(planes, *vec.shape[3:], jnp.float32)
+        + reduce_scratch(planes, w_rows, w_cols, low)
+        + reduce_scratch(planes, d_rows, down.shape[1], low)
+        + [
+            pltpu.VMEM((2, w_rows, w_cols), jnp.float32),
+            pltpu.VMEM((2, w_rows // 2, w_cols), jnp.float32),
+            pltpu.VMEM((2 * (3 + steps) + 1,) + box, jnp.float32),
+            pltpu.SemaphoreType.DMA((copies,)),
+            pltpu.SemaphoreType.DMA((copies,)),
+        ],
+        compiler_params=pltpu.CompilerParams(
+            collective_id=2, has_side_effects=True, vmem_limit_bytes=62 * 2**20
+        ),
+    )(wide, down, table, vec, conv, weight)
+
+
+def on_device_plain(
     pixels,
     sensor,
     band_wave,
@@ -144,34 +600,34 @@
     cotangent,
 ):
     fetched = (
-        lax.all_gather(pre_gain, ("dp", "fsdp"), axis=0, tiled=True),
-        lax.all_gather(pre_shift, ("dp", "fsdp"), axis=0, tiled=True),
-        lax.all_gather(qkv_weight, ("dp", "fsdp"), axis=0, tiled=True),
-        lax.all_gather(out_weight, ("dp", "fsdp"), axis=0, tiled=True),
-        lax.all_gather(mid_gain, ("dp", "fsdp"), axis=0, tiled=True),
-        lax.all_gather(mid_shift, ("dp", "fsdp"), axis=0, tiled=True),
-        lax.all_gather(up_weight, ("dp", "fsdp"), axis=0, tiled=True),
-        lax.all_gather(up_bias, ("dp", "fsdp"), axis=0, tiled=True),
-        lax.all_gather(down_weight, ("dp", "fsdp"), axis=0, tiled=True),
-        lax.all_gather(down_bias, ("dp", "fsdp"), axis=0, tiled=True),
-        lax.all_gather(dec_weight, ("dp", "fsdp"), axis=0, tiled=True),
-        lax.all_gather(dec_bias, ("dp", "fsdp"), axis=0, tiled=True),
-        lax.all_gather(mask_token, ("dp", "fsdp"), axis=0, tiled=True),
-        lax.all_gather(gen_tokens, ("dp", "fsdp"), axis=1, tiled=True),
-        lax.all_gather(gen_qkv, ("dp", "fsdp"), axis=0, tiled=True),
-        lax.all_gather(gen_out, ("dp", "fsdp"), axis=0, tiled=True),
-        lax.all_gather(gen_out_bias, ("dp", "fsdp"), axis=0, tiled=True),
-        lax.all_gather(gen_gain1, ("dp", "fsdp"), axis=0, tiled=True),
-        lax.all_gather(gen_shift1, ("dp", "fsdp"), axis=0, tiled=True),
-        lax.all_gather(gen_up, ("dp", "fsdp"), axis=0, tiled=True),
-        lax.all_gather(gen_up_bias, ("dp", "fsdp"), axis=0, tiled=True),
-        lax.all_gather(gen_down, ("dp", "fsdp"), axis=0, tiled=True),
-        lax.all_gather(gen_down_bias, ("dp", "fsdp"), axis=0, tiled=True),
-        lax.all_gather(gen_gain2, ("dp", "fsdp"), axis=0, tiled=True),
-        lax.all_gather(gen_shift2, ("dp", "fsdp"), axis=0, tiled=True),
-        lax.all_gather(kernel_weight, ("dp", "fsdp"), axis=1, tiled=True),
-        lax.all_gather(kernel_bias, ("dp", "fsdp"), axis=0, tiled=True),
-        lax.all_gather(bias_weight, ("dp", "fsdp"), axis=0, tiled=True),
+        lax.all_gather(pre_gain, AXES, axis=0, tiled=True),
+        lax.all_gather(pre_shift, AXES, axis=0, tiled=True),
+        lax.all_gather(qkv_weight, AXES, axis=0, tiled=True),
+        lax.all_gather(out_weight, AXES, axis=0, tiled=True),
+        lax.all_gather(mid_gain, AXES, axis=0, tiled=True),
+        lax.all_gather(mid_shift, AXES, axis=0, tiled=True),
+        lax.all_gather(up_weight, AXES, axis=0, tiled=True),
+        lax.all_gather(up_bias, AXES, axis=0, tiled=True),
+        lax.all_gather(down_weight, AXES, axis=0, tiled=True),
+        lax.all_gather(down_bias, AXES, axis=0, tiled=True),
+        lax.all_gather(dec_weight, AXES, axis=0, tiled=True),
+        lax.all_gather(dec_bias, AXES, axis=0, tiled=True),
+        lax.all_gather(mask_token, AXES, axis=0, tiled=True),
+        lax.all_gather(gen_tokens, AXES, axis=1, tiled=True),
+        lax.all_gather(gen_qkv, AXES, axis=0, tiled=True),
+        lax.all_gather(gen_out, AXES, axis=0, tiled=True),
+        lax.all_gather(gen_out_bias, AXES, axis=0, tiled=True),
+        lax.all_gather(gen_gain1, AXES, axis=0, tiled=True),
+        lax.all_gather(gen_shift1, AXES, axis=0, tiled=True),
+        lax.all_gather(gen_up, AXES, axis=0, tiled=True),
+        lax.all_gather(gen_up_bias, AXES, axis=0, tiled=True),
+        lax.all_gather(gen_down, AXES, axis=0, tiled=True),
+        lax.all_gather(gen_down_bias, AXES, axis=0, tiled=True),
+        lax.all_gather(gen_gain2, AXES, axis=0, tiled=True),
+        lax.all_gather(gen_shift2, AXES, axis=0, tiled=True),
+        lax.all_gather(kernel_weight, AXES, axis=1, tiled=True),
+        lax.all_gather(kernel_bias, AXES, axis=0, tiled=True),
+        lax.all_gather(bias_weight, AXES, axis=0, tiled=True),
     )
     full_kernel = fetched[25]
     full_kernel_bias = fetched[26]
@@ -264,8 +720,8 @@
     canvas = jnp.broadcast_to(full_mask, (chips, PATCH, dec_width))
     canvas = canvas.at[chip_ids, visible].set(decoded)
     ordered = jnp.take(canvas, block_order, axis=1)
-    decoder_in = lax.all_to_all(ordered, ("dp", "fsdp"), split_axis=1, concat_axis=0, tiled=True)
-    returned = lax.all_to_all(cotangent, ("dp", "fsdp"), split_axis=0, concat_axis=1, tiled=True)
+    decoder_in = lax.all_to_all(ordered, AXES, split_axis=1, concat_axis=0, tiled=True)
+    returned = lax.all_to_all(cotangent, AXES, split_axis=0, concat_axis=1, tiled=True)
     (
         full_pre_gain,
         full_pre_shift,
@@ -281,19 +737,19 @@
         full_dec_bias,
         full_mask,
     ) = (
-        lax.all_gather(pre_gain, ("dp", "fsdp"), axis=0, tiled=True),
-        lax.all_gather(pre_shift, ("dp", "fsdp"), axis=0, tiled=True),
-        lax.all_gather(qkv_weight, ("dp", "fsdp"), axis=0, tiled=True),
-        lax.all_gather(out_weight, ("dp", "fsdp"), axis=0, tiled=True),
-        lax.all_gather(mid_gain, ("dp", "fsdp"), axis=0, tiled=True),
-        lax.all_gather(mid_shift, ("dp", "fsdp"), axis=0, tiled=True),
-        lax.all_gather(up_weight, ("dp", "fsdp"), axis=0, tiled=True),
-        lax.all_gather(up_bias, ("dp", "fsdp"), axis=0, tiled=True),
-        lax.all_gather(down_weight, ("dp", "fsdp"), axis=0, tiled=True),
-        lax.all_gather(down_bias, ("dp", "fsdp"), axis=0, tiled=True),
-        lax.all_gather(dec_weight, ("dp", "fsdp"), axis=0, tiled=True),
-        lax.all_gather(dec_bias, ("dp", "fsdp"), axis=0, tiled=True),
-        lax.all_gather(mask_token, ("dp", "fsdp"), axis=0, tiled=True),
+        lax.all_gather(pre_gain, AXES, axis=0, tiled=True),
+        lax.all_gather(pre_shift, AXES, axis=0, tiled=True),
+        lax.all_gather(qkv_weight, AXES, axis=0, tiled=True),
+        lax.all_gather(out_weight, AXES, axis=0, tiled=True),
+        lax.all_gather(mid_gain, AXES, axis=0, tiled=True),
+        lax.all_gather(mid_shift, AXES, axis=0, tiled=True),
+        lax.all_gather(up_weight, AXES, axis=0, tiled=True),
+        lax.all_gather(up_bias, AXES, axis=0, tiled=True),
+        lax.all_gather(down_weight, AXES, axis=0, tiled=True),
+        lax.all_gather(down_bias, AXES, axis=0, tiled=True),
+        lax.all_gather(dec_weight, AXES, axis=0, tiled=True),
+        lax.all_gather(dec_bias, AXES, axis=0, tiled=True),
+        lax.all_gather(mask_token, AXES, axis=0, tiled=True),
     )
     restored = jnp.zeros_like(returned).at[:, block_order].set(returned)
     seen_grad = jnp.take_along_axis(restored, visible[:, :, None], axis=1)
@@ -358,7 +814,7 @@
     )
     grad_pixels = grad_pixels * valid[:, None, :, None]
     grad_kernels_part = jnp.einsum("cbw,cbk->wk", onehot, grad_band, precision=HIGH)
-    kernel_sum, grad_conv = lax.psum((grad_kernels_part, grad_conv_part), ("dp", "fsdp"))
+    kernel_sum, grad_conv = lax.psum((grad_kernels_part, grad_conv_part), AXES)
     kernel_low = kernel_sum.astype(jnp.bfloat16)
     own_low = own_part(kernel_low, 1)
     grad_kernel_weight = tdot(feature_low, own_low)
@@ -368,19 +824,19 @@
     grad_source = jnp.dot(full_bias_weight.astype(jnp.float32), grad_conv, precision=HIGH)
     core_grads = core_back((grad_feature, grad_source))
     summed = (
-        lax.psum_scatter(grad_pre_gain, ("dp", "fsdp"), scatter_dimension=0, tiled=True),
-        lax.psum_scatter(grad_pre_shift, ("dp", "fsdp"), scatter_dimension=0, tiled=True),
-        lax.psum_scatter(grad_qkv_weight, ("dp", "fsdp"), scatter_dimension=0, tiled=True),
-        lax.psum_scatter(grad_out_weight, ("dp", "fsdp"), scatter_dimension=0, tiled=True),
-        lax.psum_scatter(grad_mid_gain, ("dp", "fsdp"), scatter_dimension=0, tiled=True),
-        lax.psum_scatter(grad_mid_shift, ("dp", "fsdp"), scatter_dimension=0, tiled=True),
-        lax.psum_scatter(grad_up_weight, ("dp", "fsdp"), scatter_dimension=0, tiled=True),
-        lax.psum_scatter(grad_up_bias, ("dp", "fsdp"), scatter_dimension=0, tiled=True),
-        lax.psum_scatter(grad_down_weight, ("dp", "fsdp"), scatter_dimension=0, tiled=True),
-        lax.psum_scatter(grad_down_bias, ("dp", "fsdp"), scatter_dimension=0, tiled=True),
-        lax.psum_scatter(grad_dec_weight, ("dp", "fsdp"), scatter_dimension=0, tiled=True),
-        lax.psum_scatter(grad_dec_bias, ("dp", "fsdp"), scatter_dimension=0, tiled=True),
-        lax.psum_scatter(grad_mask, ("dp", "fsdp"), scatter_dimension=0, tiled=True),
+        lax.psum_scatter(grad_pre_gain, AXES, scatter_dimension=0, tiled=True),
+        lax.psum_scatter(grad_pre_shift, AXES, scatter_dimension=0, tiled=True),
+        lax.psum_scatter(grad_qkv_weight, AXES, scatter_dimension=0, tiled=True),
+        lax.psum_scatter(grad_out_weight, AXES, scatter_dimension=0, tiled=True),
+        lax.psum_scatter(grad_mid_gain, AXES, scatter_dimension=0, tiled=True),
+        lax.psum_scatter(grad_mid_shift, AXES, scatter_dimension=0, tiled=True),
+        lax.psum_scatter(grad_up_weight, AXES, scatter_dimension=0, tiled=True),
+        lax.psum_scatter(grad_up_bias, AXES, scatter_dimension=0, tiled=True),
+        lax.psum_scatter(grad_down_weight, AXES, scatter_dimension=0, tiled=True),
+        lax.psum_scatter(grad_down_bias, AXES, scatter_dimension=0, tiled=True),
+        lax.psum_scatter(grad_dec_weight, AXES, scatter_dimension=0, tiled=True),
+        lax.psum_scatter(grad_dec_bias, AXES, scatter_dimension=0, tiled=True),
+        lax.psum_scatter(grad_mask, AXES, scatter_dimension=0, tiled=True),
     )
     return (
         decoder_in,
@@ -416,74 +872,415 @@
     )
 
 
+def on_device(
+    pixels,
+    sensor,
+    band_wave,
+    visible,
+    block_order,
+    pre_gain,
+    pre_shift,
+    qkv_weight,
+    out_weight,
+    mid_gain,
+    mid_shift,
+    up_weight,
+    up_bias,
+    down_weight,
+    down_bias,
+    dec_weight,
+    dec_bias,
+    mask_token,
+    gen_tokens,
+    gen_qkv,
+    gen_out,
+    gen_out_bias,
+    gen_gain1,
+    gen_shift1,
+    gen_up,
+    gen_up_bias,
+    gen_down,
+    gen_down_bias,
+    gen_gain2,
+    gen_shift2,
+    kernel_weight,
+    kernel_bias,
+    bias_weight,
+    cotangent,
+):
+    arguments = (
+        pixels,
+        sensor,
+        band_wave,
+        visible,
+        block_order,
+        pre_gain,
+        pre_shift,
+        qkv_weight,
+        out_weight,
+        mid_gain,
+        mid_shift,
+        up_weight,
+        up_bias,
+        down_weight,
+        down_bias,
+        dec_weight,
+        dec_bias,
+        mask_token,
+        gen_tokens,
+        gen_qkv,
+        gen_out,
+        gen_out_bias,
+        gen_gain1,
+        gen_shift1,
+        gen_up,
+        gen_up_bias,
+        gen_down,
+        gen_down_bias,
+        gen_gain2,
+        gen_shift2,
+        kernel_weight,
+        kernel_bias,
+        bias_weight,
+        cotangent,
+    )
+    planes = lax.axis_size("dp") // 2
+    devices = planes * 8
+    if lax.axis_size("fsdp") != 4 or planes & (planes - 1) or pre_gain.shape[0] % 8:
+        return on_device_plain(*arguments)
+    low = jnp.bfloat16
+    smalls = (
+        gen_up, gen_down, bias_weight, gen_qkv, gen_out, up_bias, gen_up_bias,
+        pre_gain, pre_shift, mid_gain, mid_shift, down_bias, dec_bias, mask_token,
+        gen_out_bias, gen_gain1, gen_shift1, gen_down_bias, gen_gain2, gen_shift2, gen_tokens,
+    )
+    flat = jnp.concatenate([item.reshape(-1) for item in smalls])
+    lines = -(-flat.shape[0] // (128 * 32)) * 32
+    flat = jnp.pad(flat, (0, lines * 128 - flat.shape[0])).reshape(lines, 128)
+    spread = small_gather(flat, planes, devices).reshape(devices, lines * 128)
+    fulls = []
+    start_at = 0
+    for item in smalls[:-1]:
+        piece = spread[:, start_at : start_at + item.size]
+        start_at += item.size
+        fulls.append(piece.reshape((devices * item.shape[0],) + item.shape[1:]))
+    piece = spread[:, start_at : start_at + gen_tokens.size]
+    piece = piece.reshape(devices, gen_tokens.shape[0], gen_tokens.shape[1])
+    full_tokens = jnp.swapaxes(piece, 0, 1).reshape(gen_tokens.shape[0], -1)
+    (
+        full_gen_up, full_gen_down, full_bias_weight, full_gen_qkv, full_gen_out, full_up_bias,
+        full_gen_up_bias, full_pre_gain, full_pre_shift, full_mid_gain, full_mid_shift,
+        full_down_bias, full_dec_bias, full_mask, full_gen_out_bias, full_gain1, full_shift1,
+        full_gen_down_bias, full_gain2, full_shift2,
+    ) = fulls
+    core32 = tuple(
+        item.astype(jnp.float32)
+        for item in (
+            full_tokens, full_gen_qkv, full_gen_out, full_gen_out_bias, full_gain1, full_shift1,
+            full_gen_up, full_gen_up_bias, full_gen_down, full_gen_down_bias, full_gain2,
+            full_shift2,
+        )
+    )
+    chips, seen, bands, pix = pixels.shape
+    width = qkv_weight.shape[0] * devices
+    hidden_width = up_weight.shape[1]
+    head_dim = width // HEADS
+    scale = 1.0 / math.sqrt(head_dim)
+    dec_width = dec_weight.shape[1]
+    rows = chips * seen
+    wave_code = lax.optimization_barrier(
+        sincos(jnp.arange(NWAVE, dtype=jnp.float32), WD // 2).astype(jnp.bfloat16)
+    ).astype(jnp.float32)
+    (feature, source), core_back = jax.vjp(partial(gen_core, wave_code), *core32)
+    feature_low = feature.astype(jnp.bfloat16)
+    source_low = source.astype(jnp.bfloat16)
+    conv_bias = jnp.dot(source_low[None, :], full_bias_weight, preferred_element_type=jnp.float32)[
+        0
+    ]
+    own_table = (
+        jnp.dot(feature_low, kernel_weight, preferred_element_type=jnp.float32)
+        + kernel_bias.astype(jnp.float32)[None, :]
+    ).astype(low)
+    wide = jnp.concatenate([qkv_weight, up_weight, out_weight, dec_weight], axis=1)
+    full_wide, full_down, kernels = weight_gather(wide, down_weight, own_table, planes, devices)
+    full_down, cotangent = lax.optimization_barrier((full_down, cotangent))
+    cuts = (0, 3 * width, 3 * width + hidden_width, 4 * width + hidden_width)
+    full_qkv = full_wide[:, : cuts[1]]
+    full_up = full_wide[:, cuts[1] : cuts[2]]
+    full_out = full_wide[:, cuts[2] : cuts[3]]
+    full_dec = full_wide[:, cuts[3] :]
+    valid = band_valid(sensor, bands)
+    onehot = (band_wave[:, :, None] == jnp.arange(NWAVE, dtype=jnp.int32)[None, None, :]).astype(
+        jnp.float32
+    )
+    place = place_code(visible, width)
+    band_kernels = jnp.einsum(
+        "cbw,wk->cbk", onehot.astype(jnp.bfloat16), kernels, preferred_element_type=jnp.float32
+    ).astype(jnp.bfloat16)
+    band_kernels = band_kernels.reshape(chips, bands, pix, width)
+    masked = pixels * valid.astype(jnp.bfloat16)[:, None, :, None]
+    embedded = jnp.einsum(
+        "cvbp,cbpd->cvd", masked, band_kernels, preferred_element_type=jnp.float32
+    )
+    start = (embedded + conv_bias + place).reshape(rows, width)
+    pre_gain32 = full_pre_gain.astype(jnp.float32)
+    pre_shift32 = full_pre_shift.astype(jnp.float32)
+    normed = norm_rows(start, pre_gain32, pre_shift32).astype(jnp.bfloat16)
+    joint = jnp.dot(normed, full_qkv, preferred_element_type=jnp.float32).astype(jnp.bfloat16)
+    joint = joint.reshape(chips, seen, 3, HEADS, head_dim)
+    queries = joint[:, :, 0]
+    keys = joint[:, :, 1]
+    values = joint[:, :, 2]
+    scores = (
+        jnp.einsum("cqhe,ckhe->chqk", queries, keys, preferred_element_type=jnp.float32) * scale
+    )
+    peak = jnp.max(scores, axis=-1, keepdims=True)
+    expd = jnp.exp(scores - peak)
+    total = jnp.sum(expd, axis=-1, keepdims=True)
+    probs = (expd / total).astype(jnp.bfloat16)
+    log_total = peak + jnp.log(total)
+    context = jnp.einsum("chqk,ckhe->cqhe", probs, values, preferred_element_type=jnp.float32)
+    context = context.astype(jnp.bfloat16).reshape(rows, width)
+    attended = jnp.dot(context, full_out, preferred_element_type=jnp.float32)
+    middle = start + attended
+    mid_gain32 = full_mid_gain.astype(jnp.float32)
+    mid_shift32 = full_mid_shift.astype(jnp.float32)
+    normed2 = norm_rows(middle, mid_gain32, mid_shift32).astype(jnp.bfloat16)
+    upper = jnp.dot(normed2, full_up, preferred_element_type=jnp.float32) + full_up_bias.astype(
+        jnp.float32
+    )
+    activ = exact_gelu(upper).astype(jnp.bfloat16)
+    branch = jnp.dot(activ, full_down, preferred_element_type=jnp.float32) + full_down_bias.astype(
+        jnp.float32
+    )
+    ending = (middle + branch).astype(jnp.bfloat16)
+    decoded = jnp.dot(ending, full_dec, preferred_element_type=jnp.float32) + full_dec_bias.astype(
+        jnp.float32
+    )
+    decoded = decoded.astype(jnp.bfloat16).reshape(chips, seen, dec_width)
+    chosen = block_order[None, :, None] == visible[:, None, :]
+    choose = chosen.astype(low)
+    ordered = jnp.where(
+        jnp.any(chosen, axis=2)[:, :, None],
+        jnp.einsum("cjv,cve->cje", choose, decoded, preferred_element_type=jnp.float32).astype(low),
+        full_mask,
+    )
+    decoder_in = lax.all_to_all(ordered, AXES, split_axis=1, concat_axis=0, tiled=True)
+    returned = lax.all_to_all(cotangent, AXES, split_axis=0, concat_axis=1, tiled=True)
+    seen_grad = jnp.einsum(
+        "cjv,cje->cve", choose, returned, preferred_element_type=jnp.float32
+    ).astype(low)
+    unseen = 1.0 - jnp.any(chosen, axis=2).astype(jnp.float32)
+    grad_mask = jnp.einsum(
+        "cj,cje->e", unseen.astype(low), returned, preferred_element_type=jnp.float32
+    )
+    grad_rows = seen_grad.reshape(rows, dec_width)
+    grad_dec_weight = tdot(ending, grad_rows).astype(low)
+    grad_dec_bias = jnp.sum(grad_rows.astype(jnp.float32), axis=0)
+    grad_ending = ndot(grad_rows, full_dec)
+    grad_branch = grad_ending.astype(jnp.bfloat16)
+    grad_down_bias = jnp.sum(grad_branch.astype(jnp.float32), axis=0)
+    grad_down_weight = tdot(activ, grad_branch).astype(low)
+    grad_activ = ndot(grad_branch, full_down)
+    gelu_out, gelu_back = jax.vjp(exact_gelu, upper)
+    grad_upper = gelu_back(grad_activ)[0].astype(jnp.bfloat16)
+    grad_up_bias = jnp.sum(grad_upper.astype(jnp.float32), axis=0)
+    grad_up_weight = tdot(normed2, grad_upper).astype(low)
+    grad_normed2 = ndot(grad_upper, full_up)
+    norm_out, norm_back = jax.vjp(norm_rows, middle, mid_gain32, mid_shift32)
+    through_mid, grad_mid_gain, grad_mid_shift = norm_back(grad_normed2)
+    grad_middle = grad_ending + through_mid
+    grad_attended = grad_middle.astype(jnp.bfloat16)
+    grad_out_weight = tdot(context, grad_attended).astype(low)
+    grad_context = (
+        ndot(grad_attended, full_out).astype(jnp.bfloat16).reshape(chips, seen, HEADS, head_dim)
+    )
+    again_scores = (
+        jnp.einsum("cqhe,ckhe->chqk", queries, keys, preferred_element_type=jnp.float32) * scale
+    )
+    probs_full = jnp.exp(again_scores - log_total)
+    probs_low = probs_full.astype(jnp.bfloat16)
+    grad_values = jnp.einsum(
+        "chqk,cqhe->ckhe", probs_low, grad_context, preferred_element_type=jnp.float32
+    ).astype(jnp.bfloat16)
+    grad_probs = jnp.einsum(
+        "cqhe,ckhe->chqk", grad_context, values, preferred_element_type=jnp.float32
+    )
+    row_dot = jnp.sum(probs_full * grad_probs, axis=-1, keepdims=True)
+    grad_scores = (probs_full * (grad_probs - row_dot)).astype(jnp.bfloat16)
+    grad_queries = (
+        jnp.einsum("chqk,ckhe->cqhe", grad_scores, keys, preferred_element_type=jnp.float32) * scale
+    ).astype(jnp.bfloat16)
+    grad_keys = (
+        jnp.einsum("chqk,cqhe->ckhe", grad_scores, queries, preferred_element_type=jnp.float32)
+        * scale
+    ).astype(jnp.bfloat16)
+    grad_joint = jnp.stack([grad_queries, grad_keys, grad_values], axis=2).reshape(rows, 3 * width)
+    grad_qkv_weight = tdot(normed, grad_joint).astype(low)
+    grad_normed = ndot(grad_joint, full_qkv)
+    first_out, first_back = jax.vjp(norm_rows, start, pre_gain32, pre_shift32)
+    through_pre, grad_pre_gain, grad_pre_shift = first_back(grad_normed)
+    grad_start = grad_middle + through_pre
+    grad_conv_part = jnp.sum(grad_start, axis=0)
+    grad_embedded = grad_start.astype(jnp.bfloat16).reshape(chips, seen, width)
+    grad_band = jnp.einsum(
+        "cvbp,cvd->cbpd", masked, grad_embedded, preferred_element_type=jnp.float32
+    )
+    grad_band = grad_band.reshape(chips, bands, pix * width)
+    grad_pixels = jnp.einsum(
+        "cvd,cbpd->cvbp", grad_embedded, band_kernels, preferred_element_type=jnp.float32
+    )
+    grad_pixels = grad_pixels * valid[:, None, :, None]
+    grad_kernels_part = jnp.einsum("cbw,cbk->wk", onehot, grad_band, precision=HIGH)
+    grad_wide = jnp.concatenate(
+        [grad_qkv_weight, grad_up_weight, grad_out_weight, grad_dec_weight], axis=1
+    )
+    vectors = (
+        grad_pre_gain, grad_pre_shift, grad_mid_gain, grad_mid_shift, grad_down_bias,
+        grad_up_bias, grad_dec_bias, grad_mask,
+    )
+    vec = jnp.concatenate([item.reshape(devices, -1) for item in vectors], axis=1)
+    vec_size = vec.shape[1]
+    vec = jnp.pad(vec, ((0, 0), (0, 2048 - vec_size))).reshape(devices // 2, 2, 2, 8, 128)
+    sum_wide, sum_down, own_low, sum_vec, sum_all = grad_reduce(
+        grad_wide,
+        grad_down_weight,
+        grad_kernels_part.astype(low),
+        vec,
+        grad_conv_part.reshape(-1, 128),
+        kernel_weight,
+        planes,
+    )
+    grad_feature = sum_all[:NWAVE]
+    grad_conv = sum_all[NWAVE:].reshape(-1)
+    grad_kernel_weight = tdot(feature_low, own_low)
+    grad_kernel_bias = jnp.sum(own_low.astype(jnp.float32), axis=0)
+    grad_bias_weight = own_part(source_low.astype(jnp.float32)[:, None] * grad_conv[None, :], 0)
+    grad_source = jnp.dot(full_bias_weight.astype(jnp.float32), grad_conv, precision=HIGH)
+    core_grads = core_back((grad_feature, grad_source))
+    sum_vec = sum_vec.reshape(-1)
+    vec_out = []
+    at = 0
+    for item in vectors:
+        vec_out.append(sum_vec[at : at + item.shape[0] // devices])
+        at += item.shape[0] // devices
+    summed = (
+        vec_out[0],
+        vec_out[1],
+        sum_wide[:, : cuts[1]],
+        sum_wide[:, cuts[2] : cuts[3]],
+        vec_out[2],
+        vec_out[3],
+        sum_wide[:, cuts[1] : cuts[2]],
+        vec_out[5],
+        sum_down,
+        vec_out[4],
+        sum_wide[:, cuts[3] :],
+        vec_out[6],
+        vec_out[7],
+    )
+    return (
+        decoder_in,
+        grad_pixels,
+        summed[0],
+        summed[1],
+        summed[2],
+        summed[3],
+        summed[4],
+        summed[5],
+        summed[6],
+        summed[7],
+        summed[8],
+        summed[9],
+        summed[10],
+        summed[11],
+        summed[12],
+        own_part(core_grads[0], 1),
+        own_part(core_grads[1], 0),
+        own_part(core_grads[2], 0),
+        own_part(core_grads[3], 0),
+        own_part(core_grads[4], 0),
+        own_part(core_grads[5], 0),
+        own_part(core_grads[6], 0),
+        own_part(core_grads[7], 0),
+        own_part(core_grads[8], 0),
+        own_part(core_grads[9], 0),
+        own_part(core_grads[10], 0),
+        own_part(core_grads[11], 0),
+        grad_kernel_weight,
+        grad_kernel_bias,
+        grad_bias_weight,
+    )
+
+
 def solution(mesh):
     in_specs = (
-        P(("dp", "fsdp"), None, None, None),
-        P(("dp", "fsdp")),
-        P(("dp", "fsdp"), None),
-        P(("dp", "fsdp"), None),
+        P(AXES, None, None, None),
+        P(AXES),
+        P(AXES, None),
+        P(AXES, None),
         P(),
-        P(("dp", "fsdp")),
-        P(("dp", "fsdp")),
-        P(("dp", "fsdp"), None),
-        P(("dp", "fsdp"), None),
-        P(("dp", "fsdp")),
-        P(("dp", "fsdp")),
-        P(("dp", "fsdp"), None),
-        P(("dp", "fsdp")),
-        P(("dp", "fsdp"), None),
-        P(("dp", "fsdp")),
-        P(("dp", "fsdp"), None),
-        P(("dp", "fsdp")),
-        P(("dp", "fsdp")),
-        P(None, ("dp", "fsdp")),
-        P(("dp", "fsdp"), None),
-        P(("dp", "fsdp"), None),
-        P(("dp", "fsdp")),
-        P(("dp", "fsdp")),
-        P(("dp", "fsdp")),
-        P(("dp", "fsdp"), None),
-        P(("dp", "fsdp")),
-        P(("dp", "fsdp"), None),
-        P(("dp", "fsdp")),
-        P(("dp", "fsdp")),
-        P(("dp", "fsdp")),
-        P(None, ("dp", "fsdp")),
-        P(("dp", "fsdp")),
-        P(("dp", "fsdp"), None),
-        P(None, ("dp", "fsdp"), None),
+        P(AXES),
+        P(AXES),
+        P(AXES, None),
+        P(AXES, None),
+        P(AXES),
+        P(AXES),
+        P(AXES, None),
+        P(AXES),
+        P(AXES, None),
+        P(AXES),
+        P(AXES, None),
+        P(AXES),
+        P(AXES),
+        P(None, AXES),
+        P(AXES, None),
+        P(AXES, None),
+        P(AXES),
+        P(AXES),
+        P(AXES),
+        P(AXES, None),
+        P(AXES),
+        P(AXES, None),
+        P(AXES),
+        P(AXES),
+        P(AXES),
+        P(None, AXES),
+        P(AXES),
+        P(AXES, None),
+        P(None, AXES, None),
     )
     out_specs = (
-        P(None, ("dp", "fsdp"), None),
-        P(("dp", "fsdp"), None, None, None),
-        P(("dp", "fsdp")),
-        P(("dp", "fsdp")),
-        P(("dp", "fsdp"), None),
-        P(("dp", "fsdp"), None),
-        P(("dp", "fsdp")),
-        P(("dp", "fsdp")),
-        P(("dp", "fsdp"), None),
-        P(("dp", "fsdp")),
-        P(("dp", "fsdp"), None),
-        P(("dp", "fsdp")),
-        P(("dp", "fsdp"), None),
-        P(("dp", "fsdp")),
-        P(("dp", "fsdp")),
-        P(None, ("dp", "fsdp")),
-        P(("dp", "fsdp"), None),
-        P(("dp", "fsdp"), None),
-        P(("dp", "fsdp")),
-        P(("dp", "fsdp")),
-        P(("dp", "fsdp")),
-        P(("dp", "fsdp"), None),
-        P(("dp", "fsdp")),
-        P(("dp", "fsdp"), None),
-        P(("dp", "fsdp")),
-        P(("dp", "fsdp")),
-        P(("dp", "fsdp")),
-        P(None, ("dp", "fsdp")),
-        P(("dp", "fsdp")),
-        P(("dp", "fsdp"), None),
+        P(None, AXES, None),
+        P(AXES, None, None, None),
+        P(AXES),
+        P(AXES),
+        P(AXES, None),
+        P(AXES, None),
+        P(AXES),
+        P(AXES),
+        P(AXES, None),
+        P(AXES),
+        P(AXES, None),
+        P(AXES),
+        P(AXES, None),
+        P(AXES),
+        P(AXES),
+        P(None, AXES),
+        P(AXES, None),
+        P(AXES, None),
+        P(AXES),
+        P(AXES),
+        P(AXES),
+        P(AXES, None),
+        P(AXES),
+        P(AXES, None),
+        P(AXES),
+        P(AXES),
+        P(AXES),
+        P(None, AXES),
+        P(AXES),
+        P(AXES, None),
     )
     return jax.shard_map(
         on_device, mesh=mesh, in_specs=in_specs, out_specs=out_specs, check_vma=False

time: 1270 us -> 546 us (0.43); the launches traced: 1250 us -> 541 us
  blocking collectives: 550 us -> 0 us
  Pallas kernels: 0 us -> 232 us
  waiting for transfers between devices: 228 us -> 0.01 us
  local copies, waits for them, and re-layouts: 242 us -> 113 us
  matrix products: 164 us -> 140 us
  between operations: 16.5 us -> 2.89 us
    all_gather x8 -> x0, blocking collectives: 363 us -> none  [the longest x1 85.2 us: on_device(): lax.all_gather(gen_tokens, ('dp', 'fsdp'), axis=1, tiled=True)]
    pallas_call x0 -> x3, Pallas kernels: none -> 232 us  [the longest x1 113 us: grad_reduce(): pl.pallas_call(partial(grad_reduce_kernel, planes, steps), out_shape=(jax...]
    reduce_scatter x5 -> x0, waiting for transfers between devices: 225 us -> none  [the longest x1 142 us: on_device(): lax.psum_scatter(grad_down_weight, ('dp', 'fsdp'), scatter_dimension=0, t...]
    unnamed x2 -> x0, blocking collectives: 187 us -> none
    scatter x4 -> x0, local copies, waits for them, and re-layouts: 145 us -> none  [the longest x2 75.6 us: on_device(): restored = jnp.zeros_like(returned).at[:, block_order].set(returned)]
    gather x2 -> x0, local copies, waits for them, and re-layouts: 14.8 us -> none  [the longest x1 7.47 us: on_device(): ordered = jnp.take(canvas, block_order, axis=1)]
    unnamed x299 -> x249, local copies, waits for them, and re-layouts: 28.1 us -> 17.2 us
    dot_general x6 -> x5, matrix products: 32 us -> 21.5 us  [ndot(): lax.dot_general(left, right, (((1,), (1,)), ((), ())), preferred_element_...]
  transfers between devices with their start and end apart: 12 -> 2, of which waited for: 2 -> 0; matrix products, arithmetic and copies ran while one was open for 34% -> 43% of each run, Pallas kernels for 0% -> 21%
where the time goes in v1:
time: 546 us; the launch traced here: 541 us
  Pallas kernels  232 us (42%)
  matrix products  140 us (26%)
  local copies, waits for them, and re-layouts  113 us (21%)
  other arithmetic  33.1 us (6%)
  starting transfers between devices  21 us (4%)
    pallas_call x1, Pallas kernels, grad_reduce(): pl.pallas_call(partial(grad_reduce_kernel, planes, steps), out_shape=(jax...  113 us
    pallas_call x1, Pallas kernels, weight_gather(): pl.pallas_call(partial(weight_gather_kernel, planes), out_shape=(jax.Shap...  93.5 us
    pallas_call x1, Pallas kernels, small_gather(): pl.pallas_call(partial(small_gather_kernel, planes), out_shape=jax.ShapeD...  25.7 us
    dot_general x5, matrix products, ndot(): lax.dot_general(left, right, (((1,), (1,)), ((), ())), preferred_element_...  21.5 us
    dot_general x6, matrix products, tdot(): lax.dot_general(left, right, (((0,), (0,)), ((), ())), preferred_element_...  20.1 us
    dot_general x1, matrix products, on_device(): jnp.dot(normed2, full_up, preferred_element_type=jnp.float32)  18 us
    unnamed x249, local copies, waits for them, and re-layouts  17.2 us
    all_to_all x1, starting transfers between devices, on_device(): lax.all_to_all(cotangent, AXES, split_axis=0, concat_axis=1, tiled=True)  14.6 us
  transfers between devices with their start and end apart: 2, of which 0 were waited for; matrix products, arithmetic and copies ran while one was open for 43% of the time, Pallas kernels for 21%

profile of v1, /device:TPU:0, one launch (start us, length us, event | category | flops | bytes accessed | tf_op | source)
XLA Modules:
  0.0 541.1 jit_solution(15274906179001997462)
XLA Ops:
  3.7 11.5 %concatenate.23 = bf16[22356]{0:T(1024)(128)(2,1)S(1)} concatenate(bf16[8192]{0:T(1024)(128)(2,1)S(1)} %bitcast.264, bf16[8192]{0:T(1024)(128)(2,1)} %bitcast.272, bf16[3072]{0:T(1024)(128)(2,1)S(1)} %reshape.587, bf16[1536]{0:T(1024)(128)(2,1)S(1)} %reshape.588, bf16[512]{0:T(512)(128)(2,1)} %bitcast.277, bf16[96]{0:T(256)(128)(2,1)} %param.47, bf16[64]{0:T(256)(128)(2,1)} %param.60, ...), dimensions={0} | concatenate | bytes 89424 | tf_op jit(solution)/shard_map/concatenate | solution.py:957
  15.9 25.7 %shard_map.562 = bf16[32,192,128]{2,1,0:T(8,128)(2,1)} custom-call(bf16[192,128]{1,0:T(8,128)(2,1)} %pad_bitcast_fusion.1.src), custom_call_target="tpu_custom_call" | custom-call | tf_op jit(solution)/shard_map/pallas_call | solution.py:265
  57.5 93.5 %shard_map.563 = (bf16[768,6656]{1,0:T(8,128)(2,1)}, bf16[3072,768]{1,0:T(8,128)(2,1)S(1)}, bf16[32,49152]{1,0:T(8,128)(2,1)S(1)}) custom-call(bf16[24,6656]{1,0:T(8,128)(2,1)S(1)} %pad_maximum_fusion.2.wide, bf16[96,768]{1,0:T(8,128)(2,1)S(1)} %copy-done, bf16[32,1536]{1,0:T(8,128)(2,1)S(1)} %fusion.27.table), custom_call_target="tpu_custom_call" | custom-call | tf_op jit(solution)/shard_map/pallas_call | solution.py:349
  153.2 14.6 %all-to-all-start.1 = ((bf16[64,32,512]{2,1,0:T(8,128)(2,1)}), bf16[64,32,512]{2,1,0:T(8,128)(2,1)}, u32[]{:S(2)}, u32[]{:S(2)}) async-start(bf16[64,32,512]{2,1,0:T(8,128)(2,1)} %param.68), calls=%async_computation.1 | async-start | bytes 4194304 | tf_op jit(solution)/shard_map/all_to_all | solution.py:1069
  180.3 4.7 reshape.650
  192.5 5.4 convolution_convert_fusion.4
  197.9 4.3 copy.166
  202.3 6.0 %reshape.602 = bf16[2,256,3,12,64]{1,0,4,3,2:T(2,128)(2,1)} reshape(bf16[512,2304]{0,1:T(8,128)(2,1)} %copy.166) | data formatting | bytes 4718592 | tf_op jit(solution)/shard_map/reshape | solution.py:1030
  208.3 14.4 %fusion.140 = (bf16[2,256,1,12,64]{1,0,4,3,2:T(2,128)(2,1)S(1)}, bf16[2,256,1,12,64]{1,0,4,3,2:T(2,128)(2,1)S(1)}, bf16[2,256,1,12,64]{1,0,4,3,2:T(2,128)(2,1)S(1)}) fusion(bf16[2,256,3,12,64]{1,0,4,3,2:T(2,128)(2,1)} %reshape.602), kind=kLoop, calls=%fused_computation.299 | loop fusion | bytes 4718592 | tf_op jit(solution)/shard_map/slice | solution.py:1033
  231.6 18.0 %multiply_convert_fusion.1 = (bf16[512,3072]{1,0:T(8,128)(2,1)}, f32[512,3072]{1,0:T(8,128)}, f32[512,3072]{1,0:T(8,128)}) fusion(f32[3072]{0:T(1024)S(1)} %copy-done.84, bf16[768,6656]{1,0:T(8,128)(2,1)S(1)} %bitcast.262, f32[512,768]{1,0:T(8,128)S(1)} %get-tuple-element.250, f32[768]{0:T(1024)S(1)} %copy-done.101, f32[768]{0:T(1024)S(1)} %copy-done.81, ...), kind=kOutput, calls=%fused_computation.12 | convolution fusion | flops 2521694208 | bytes 22044672 | tf_op jit(solution)/shard_map/dot_general | solution.py:1049
  251.2 5.9 %add_convert_fusion.2 = bf16[512,768]{1,0:T(8,128)(2,1)S(1)} fusion(f32[512,768]{1,0:T(8,128)S(1)} %get-tuple-element.250, bf16[512,3072]{1,0:T(8,128)(2,1)} %get-tuple-element.190, bf16[3072,768]{1,0:T(8,128)(2,1)} %copy-done.1, f32[768]{0:T(1024)S(1)} %reshape.635), kind=kOutput, calls=%fused_computation.77 | convolution fusion | flops 2417098752 | bytes 10226688 | tf_op jit(solution)/shard_map/dot_general | solution.py:1053
  265.9 6.3 %all-to-all-start = ((bf16[2,1024,512]{2,0,1:T(2,128)(2,1)}), bf16[2,1024,512]{2,0,1:T(2,128)(2,1)}, u32[]{:S(2)}, u32[]{:S(2)}) async-start(bf16[2,1024,512]{2,0,1:T(2,128)(2,1)} %copy.173), calls=%async_computation | async-start | bytes 4194304 | tf_op jit(solution)/shard_map/all_to_all | solution.py:1068
  278.3 4.3 convolution_convert_fusion.1.refs_1_
  282.6 7.6 %convert_reduce_fusion = (f32[3072]{0:T(1024)S(1)}, bf16[512,3072]{1,0:T(8,128)(2,1)S(1)}) fusion(f32[512,3072]{1,0:T(8,128)} %get-tuple-element.191, bf16[3072,768]{1,0:T(8,128)(2,1)S(1)} %bitcast.224, f32[512,768]{1,0:T(8,128)S(1)} %fusion.66, f32[512,3072]{1,0:T(8,128)} %get-tuple-element.251, f32[3072]{0:T(1024)S(1)} %copy-done.84), kind=kOutput, calls=%fused_computation.7 | convolution fusion | flops 2443047936 | bytes 22044672 | tf_op jit(solution)/shard_map/dot_general | solution.py:108
  290.2 5.3 multiply_reduce_fusion.2
  295.5 4.9 convolution_convert_fusion.2
  309.9 5.1 fusion.49
  330.7 4.4 multiply_reduce_fusion.3
  341.0 5.7 %convolution_convert_fusion.3 = bf16[768,2304]{1,0:T(8,128)(2,1)} fusion(bf16[512,768]{1,0:T(8,128)(2,1)S(1)} %bitcast.255, bf16[512,2304]{0,1:T(8,128)(2,1)} %bitcast.249), kind=kOutput, calls=%fused_computation.32 | convolution fusion | flops 1813708800 | bytes 6684672 | tf_op jit(solution)/shard_map/dot_general | solution.py:102
  351.0 8.0 %reshape.610 = f32[2,13,49152]{2,0,1:T(2,128)} reshape(f32[2,13,64,768]{3,2,0,1:T(8,128)} %fusion.60) | data formatting | bytes 10223616 | tf_op jit(solution)/shard_map/reshape | solution.py:1129
  359.0 10.6 %fusion.refs_2_ = bf16[32,49152]{1,0:T(8,128)(2,1)} fusion(f32[2,13,49152]{2,0,1:T(2,128)} %reshape.610, s32[2,13]{1,0:T(2,128)S(1)} %copy-done.85), kind=kOutput, calls=%fused_computation.1 | convolution fusion | flops 492307264 | bytes 8257640 | tf_op jit(solution)/shard_map/cbw,cbk->wk/dot_general | solution.py:1134
  369.7 11.4 %pad_maximum_fusion.refs_0_ = bf16[768,6656]{1,0:T(8,128)(2,1)} fusion(bf16[768,512]{1,0:T(8,128)(2,1)S(1)} %copy-done.48, bf16[768,768]{1,0:T(8,128)(2,1)S(1)} %copy-done.23, bf16[768,3072]{1,0:T(8,128)(2,1)} %convolution_convert_fusion.2, bf16[768,2304]{1,0:T(8,128)(2,1)S(1)} %copy-done.24), kind=kLoop, calls=%fused_computation.3 | loop fusion | flops 40894464 | bytes 20447232 | tf_op jit(solution)/shard_map/concatenate | solution.py:1135
  381.2 112.7 %shard_map.564 = (f32[24,6656]{1,0:T(8,128)}, f32[96,768]{1,0:T(8,128)}, bf16[32,1536]{1,0:T(8,128)(2,1)}, f32[2,8,128]{2,1,0:T(8,128)}, f32[38,128]{1,0:T(8,128)}) custom-call(bf16[768,6656]{1,0:T(8,128)(2,1)} %pad_maximum_fusion.refs_0_, bf16[3072,768]{1,0:T(8,128)(2,1)} %convolution_convert_fusion.1.refs_1_, bf16[32,49152]{1,0:T(8,128)(2,1)} %fusion.refs_2_, ...), custom_call_target="tpu_custom_call" | custom-call | tf_op jit(solution)/shard_map/pallas_call | solution.py:538
  519.6 4.7 fusion.69
  (438 shorter events, 143.0 us)
Async XLA Ops:
  45.0 11.8 %copy-start.61 = (bf16[32,128]{1,0:T(8,128)(2,1)}, bf16[32,128]{1,0:T(8,128)(2,1)S(1)}, u32[]{:S(2)}) copy-start(bf16[32,128]{1,0:T(8,128)(2,1)S(1)} %pad_maximum_fusion.6) | copy-start | bytes 24580
  153.1 17.8 %copy-start.107 = (s32[2]{0:T(128)S(1)}, s32[2]{0:T(128)}, u32[]{:S(2)}) copy-start(s32[2]{0:T(128)} %param.36) | copy-start | bytes 28
  153.1 17.8 %copy-start.108 = (s32[4]{0:T(128)S(1)}, s32[4]{0:T(128)}, u32[]{:S(2)}) copy-start(s32[4]{0:T(128)} %constant.200.clone) | copy-start | bytes 52
  153.2 18.7 %copy-start.92 = (s32[2,256]{1,0:T(2,128)S(1)}, s32[2,256]{1,0:T(2,128)}, u32[]{:S(2)}) copy-start(s32[2,256]{1,0:T(2,128)} %param.38) | copy-start | bytes 6148
  153.2 112.8 %all-to-all-start.1 = ((bf16[64,32,512]{2,1,0:T(8,128)(2,1)}), bf16[64,32,512]{2,1,0:T(8,128)(2,1)}, u32[]{:S(2)}, u32[]{:S(2)}) async-start(bf16[64,32,512]{2,1,0:T(8,128)(2,1)} %param.68), calls=%async_computation.1 | async-start | bytes 4194304 | tf_op jit(solution)/shard_map/all_to_all | solution.py:1069
  191.8 72.9 %copy-start.3 = (f32[2,256,768]{2,1,0:T(8,128)}, f32[2,256,768]{2,1,0:T(8,128)S(1)}, u32[]{:S(2)}) copy-start(f32[2,256,768]{2,1,0:T(8,128)S(1)} %get-tuple-element.246) | copy-start | bytes 4718596
  231.6 18.1 %copy-start.55 = (bf16[32,512]{1,0:T(8,128)(2,1)S(1)}, bf16[32,512]{1,0:T(8,128)(2,1)}, u32[]{:S(2)}) copy-start(bf16[32,512]{1,0:T(8,128)(2,1)} %copy-done.54) | copy-start | bytes 98308
  231.6 19.2 %copy-start.93 = (s32[2,256]{1,0:T(2,128)S(1)}, s32[2,256]{1,0:T(2,128)}, u32[]{:S(2)}) copy-start(s32[2,256]{1,0:T(2,128)} %param.38) | copy-start | bytes 6148
  231.6 19.2 %copy-start.102 = (s32[1024]{0:T(1024)S(1)}, s32[1024]{0:T(1024)}, u32[]{:S(2)}) copy-start(s32[1024]{0:T(1024)} %param.39) | copy-start | bytes 12292
  265.9 258.3 %all-to-all-start = ((bf16[2,1024,512]{2,0,1:T(2,128)(2,1)}), bf16[2,1024,512]{2,0,1:T(2,128)(2,1)}, u32[]{:S(2)}, u32[]{:S(2)}) async-start(bf16[2,1024,512]{2,0,1:T(2,128)(2,1)} %copy.173), calls=%async_computation | async-start | bytes 4194304 | tf_op jit(solution)/shard_map/all_to_all | solution.py:1068
  304.0 10.9 %slice-start.2 = ((s8[6291456]{0:T(1024)(128)(4,1)}), s8[2097152]{0:T(1024)(128)(4,1)S(1)}, s32[]{:S(2)}) async-start(s8[6291456]{0:T(1024)(128)(4,1)} %bitcast.225), calls=%async_computation.4 | async-start | bytes 4194304
  359.0 10.7 %copy-start.24 = (bf16[768,2304]{1,0:T(8,128)(2,1)S(1)}, bf16[768,2304]{1,0:T(8,128)(2,1)}, u32[]{:S(2)}) copy-start(bf16[768,2304]{1,0:T(8,128)(2,1)} %convolution_convert_fusion.3) | copy-start | bytes 10616836
  381.1 120.4 %copy-start.38 = (bf16[128,768]{1,0:T(8,128)(2,1)S(1)}, bf16[128,768]{1,0:T(8,128)(2,1)}, u32[]{:S(2)}) copy-start(bf16[128,768]{1,0:T(8,128)(2,1)} %copy-done.37) | copy-start | bytes 589828
  381.1 120.7 %copy-start.32 = (f32[161,128]{1,0:T(8,128)S(1)}, f32[161,128]{1,0:T(8,128)}, u32[]{:S(2)}) copy-start(f32[161,128]{1,0:T(8,128)} %copy-done.31) | copy-start | bytes 247300
  381.1 120.7 %copy-start.75 = (f32[161]{0:T(256)S(1)}, f32[161]{0:T(256)}, u32[]{:S(2)}) copy-start(f32[161]{0:T(256)} %copy-done.74) | copy-start | bytes 1936
  381.1 120.7 %copy-start.78 = (f32[161]{0:T(256)S(1)}, f32[161]{0:T(256)}, u32[]{:S(2)}) copy-start(f32[161]{0:T(256)} %copy-done.77) | copy-start | bytes 1936
  381.1 120.7 %copy-start.91 = (f32[128]{0:T(128)S(1)}, f32[128]{0:T(128)}, u32[]{:S(2)}) copy-start(f32[128]{0:T(128)} %copy-done.90) | copy-start | bytes 1540
  381.1 120.9 %copy-start.89 = (f32[161]{0:T(256)S(1)}, f32[161]{0:T(256)}, u32[]{:S(2)}) copy-start(f32[161]{0:T(256)} %copy-done.88) | copy-start | bytes 1936
  381.1 121.2 %copy-start.36 = (bf16[2048,128]{1,0:T(8,128)(2,1)S(1)}, bf16[2048,128]{1,0:T(8,128)(2,1)}, u32[]{:S(2)}) copy-start(bf16[2048,128]{1,0:T(8,128)(2,1)} %copy-done.35) | copy-start | bytes 1572868
  524.3 13.1 %slice-start.7 = ((f32[161,128]{1,0:T(8,128)}), f32[1,128]{1,0:T(1,128)S(1)}, s32[]{:S(2)}) async-start(f32[161,128]{1,0:T(8,128)} %copy-done.56), calls=%async_computation.9 | async-start | bytes 1024 | tf_op jit(solution)/shard_map/transpose(jvp())/split | solution.py:73
  524.3 13.1 %slice-start.8 = ((f32[161,128]{1,0:T(8,128)}), f32[129,128]{1,0:T(8,128)S(1)}, s32[]{:S(2)}) async-start(f32[161,128]{1,0:T(8,128)} %copy-done.56), calls=%async_computation.10 | async-start | bytes 139264 | tf_op jit(solution)/shard_map/slice
  524.3 13.1 %copy-start.106 = (pred[129]{0:T(512)(128)(4,1)S(1)}, pred[129]{0:T(512)(128)(4,1)}, u32[]{:S(2)}) copy-start(pred[129]{0:T(512)(128)(4,1)} %constant.192.clone.1) | copy-start | bytes 391
  524.3 13.9 %copy-start.7 = (bf16[2,13,64,768]{3,2,1,0:T(8,128)(2,1)S(1)}, bf16[2,13,64,768]{3,2,1,0:T(8,128)(2,1)}, u32[]{:S(2)}) copy-start(bf16[2,13,64,768]{3,2,1,0:T(8,128)(2,1)} %reshape.650) | copy-start | bytes 7667716
  524.3 13.8 %copy-start.71 = (f32[2,13]{1,0:T(2,128)S(1)}, f32[2,13]{1,0:T(2,128)}, u32[]{:S(2)}) copy-start(f32[2,13]{1,0:T(2,128)} %get-tuple-element.233) | copy-start | bytes 316
  (99 other events, 348.1 us)
